TPU v7x, 32 devices: a whole 2x2x4 slice. The times are simulated.
32 devices in a mesh: dp: 8 (over z, y), expert: 4 (over x, core).
Axes of the slice: x: 2, y: 2, z: 4, core: 2. Of those that a mesh axis runs over, the one named last changes fastest.
Arguments:
- tokens: bfloat16 [16384, 768], P(('dp', 'expert')), may hold values from -6 to 6
- assigned: int32 [16384, 1], P(('dp', 'expert')), may hold values from 0 to 3; in each aligned block of 512 rows (0 to 511, 512 to 1023, ...) at most 256 rows name the same one
- gate_prob: float32 [16384, 1], P(('dp', 'expert')), may hold values from 0.2 to 1
- cotangent: bfloat16 [16384, 768], P(('dp', 'expert')), may hold values from -6 to 6
- weight_in: bfloat16 [4, 768, 3072], P('expert'), may hold values from -0.21875 to 0.21875
- weight_out: bfloat16 [4, 3072, 768], P('expert'), may hold values from -0.109375 to 0.109375
- moment_in: float32 [4, 768, 3072], P('expert', 'dp'), may hold values from -60 to 60
- moment_out: float32 [4, 3072, 768], P('expert', 'dp'), may hold values from -60 to 60
- second_in: float32 [4, 768, 3072], P('expert', 'dp'), may hold values from 1 to 1000
- second_out: float32 [4, 3072, 768], P('expert', 'dp'), may hold values from 1 to 1000
Outputs:
- combined: bfloat16 [16384, 768], P(('dp', 'expert'))
- new_weight_in: float32 [4, 768, 3072], P('expert', 'dp')
- new_weight_out: float32 [4, 3072, 768], P('expert', 'dp')
- new_moment_in: float32 [4, 768, 3072], P('expert', 'dp')
- new_moment_out: float32 [4, 3072, 768], P('expert', 'dp')
- new_second_in: float32 [4, 768, 3072], P('expert', 'dp')
- new_second_out: float32 [4, 3072, 768], P('expert', 'dp')
Inputs may be any that keep to these rules, and one draw needn't show every extreme that they name: `assigned`: within each device's 512 rows (aligned blocks), no expert is named more than 256 times, a bound that some block reaches; every expert is named somewhere.
All inputs are finite; a program needn't handle non-finite values.
Results may differ from a plain program's by a relative error of at most 0.0012.
The roundings to bfloat16 on the way count: a program that leaves them out, or rounds other values in their place, can miss the bound.
Values may be sent and summed in bfloat16 or wider, within the bound.
No kernel may reach another device: no remote copies, remote signals or barrier semaphores. Data moves between devices by JAX's collectives and lax.ppermute only.
A program may use at most 192 MiB of HBM per device.

v0:
```python
import functools

import jax
import jax.numpy as jnp
from jax import lax
from jax.experimental import pallas as pl
from jax.experimental.pallas import tpu as pltpu
from jax.sharding import PartitionSpec as P

eps_adasum = 1e-06
f32 = jnp.float32
bf16 = jnp.bfloat16
f16 = jnp.float16
VMEM_LIMIT = 48 << 20


def swap(x, axis, offset):
    return lax.ppermute(x, axis, [(i, i ^ offset) for i in range(lax.axis_size(axis))])


def gelu_and_slope(values):
    root = 0.7978845608028654
    square = values * values
    tanh = jnp.tanh(values * (root + (root * 0.044715) * square))
    cdf = 0.5 + 0.5 * tanh
    slope = cdf + (0.5 * values) * (1.0 - tanh * tanh) * (root + (3.0 * root * 0.044715) * square)
    return values * cdf, slope


def adam_update(grad, weight, moment, second):
    new_moment = 0.9 * moment + 0.1 * grad
    new_second = 0.999 * second + 0.001 * grad * grad
    corr_one = 1.0 - 0.9**10.0
    corr_two = 1.0 - 0.999**10.0
    update = new_moment / corr_one / (jnp.sqrt(new_second / corr_two) + 1e-08)
    return (weight - 0.001 * update, new_moment, new_second)


def contract_rows(left, right):
    return lax.dot_general(
        left, right, (((0,), (0,)), ((), ())), preferred_element_type=f32
    )


def slot_table(assigned, expert, experts, capacity):
    expert_ids = assigned[:, 0]
    one_hot = (expert_ids[:, None] == jnp.arange(experts, dtype=jnp.int32)[None, :]).astype(
        jnp.int32
    )
    slot_index = jnp.sum((jnp.cumsum(one_hot, axis=0) - one_hot) * one_hot, axis=1)
    slot_code = (expert_ids ^ expert) * capacity + slot_index
    rows = experts * capacity
    return (jnp.arange(rows, dtype=jnp.int32)[:, None] == slot_code[None, :]).astype(bf16)


def exchange_blocks(blocks):
    return [blocks[0]] + [swap(blocks[j], "expert", j) for j in range(1, len(blocks))]


def dispatch(table, rows, experts):
    capacity = table.shape[0] // experts
    sent = jnp.dot(table, rows, preferred_element_type=f32).astype(bf16)
    blocks = [sent[j * capacity : (j + 1) * capacity] for j in range(experts)]
    return jnp.concatenate(exchange_blocks(blocks), axis=0)


def fold(values):
    rows = values.reshape(values.shape[0] // 8, 8, values.shape[1]).sum(0)
    spare = -rows.shape[1] % 128
    if spare:
        rows = jnp.concatenate([rows, jnp.zeros((8, spare), f32)], axis=1)
    return sum(rows[:, k * 128 : (k + 1) * 128] for k in range(rows.shape[1] // 128))


def expert_kernel(half_ref, x_ref, u_ref, w1_ref, w2_ref, *rest, steps, own):
    if own:
        out_ref, gi_ref, go_ref, xt_ref, ut_ref, acc_ref = rest
    else:
        own_gi_ref, own_go_ref, gi_ref, go_ref, stat_ref, xt_ref, ut_ref, acc_ref = rest
    step = pl.program_id(0)
    half_width = xt_ref.shape[0]

    @pl.when(step == 0)
    def _():
        start = pl.multiple_of(half_ref[0] * half_width, half_width)
        xt_ref[...] = x_ref[:, pl.ds(start, half_width)].T
        ut_ref[...] = u_ref[...].T

    pre = jnp.dot(x_ref[...], w1_ref[...], preferred_element_type=f32)
    back = lax.dot_general(
        u_ref[...], w2_ref[...], (((1,), (1,)), ((), ())), preferred_element_type=f32
    )
    act, slope = gelu_and_slope(pre)
    hidden = act.astype(bf16)
    hidden_grad = (slope * back).astype(bf16)
    gi_ref[...] = jnp.dot(xt_ref[...], hidden_grad, preferred_element_type=f32)

    @pl.when(step < steps // 2)
    def _():
        go_ref[...] = jnp.dot(ut_ref[...], hidden, preferred_element_type=f32)

    if own:
        product = jnp.dot(hidden, w2_ref[...], preferred_element_type=f32)

        @pl.when(step == 0)
        def _():
            acc_ref[...] = product

        @pl.when(step > 0)
        def _():
            acc_ref[...] += product

        @pl.when(step == steps - 1)
        def _():
            out_ref[...] = acc_ref[...].astype(bf16)

    else:

        def add(mine, far):
            acc_ref[0] += fold(mine * far)
            acc_ref[1] += fold(mine * mine)
            acc_ref[2] += fold(far * far)

        @pl.when(step == 0)
        def _():
            acc_ref[...] = jnp.zeros_like(acc_ref)

        add(own_gi_ref[...], gi_ref[...])

        @pl.when(step < steps // 2)
        def _():
            add(own_go_ref[...], go_ref[...])

        @pl.when(step == steps - 1)
        def _():
            row = lax.broadcasted_iota(jnp.int32, (8, 128), 0)
            stats = jnp.zeros((8, 128), f32)
            for k in range(3):
                stats = jnp.where(row == k, jnp.sum(acc_ref[k]), stats)
            stat_ref[...] = stats


def expert_call(half, x, u, w1, w2, previous):
    rows, width = x.shape
    hidden_width = w1.shape[1]
    steps = 6
    block = hidden_width // steps
    own = previous is None

    def column(i, h):
        return (0, (i + h[0] * (steps // 2)) % steps)

    def row(i, h):
        return ((i + h[0] * (steps // 2)) % steps, 0)

    def held(i, h):
        return (0, jnp.minimum(i, steps // 2 - 1))

    def whole(i, h):
        return (0, 0)

    one = pl.Buffered(1)
    in_specs = [
        pl.BlockSpec((rows, width), whole, pipeline_mode=one),
        pl.BlockSpec((rows, width), whole, pipeline_mode=one),
        pl.BlockSpec((width, block), column),
        pl.BlockSpec((block, width), row),
    ]
    grad_specs = [pl.BlockSpec((width // 2, block), column), pl.BlockSpec((width, block), held)]
    grad_shapes = [
        jax.ShapeDtypeStruct((width // 2, hidden_width), f32),
        jax.ShapeDtypeStruct((width, hidden_width // 2), f32),
    ]
    scratch = [pltpu.VMEM((width // 2, rows), bf16), pltpu.VMEM((width, rows), bf16)]
    args = [x, u, w1, w2]
    if own:
        out_specs = [pl.BlockSpec((rows, width), whole)] + grad_specs
        out_shape = [jax.ShapeDtypeStruct((rows, width), bf16)] + grad_shapes
        scratch.append(pltpu.VMEM((rows, width), f32))
    else:
        in_specs += grad_specs
        args += list(previous)
        out_specs = grad_specs + [pl.BlockSpec((8, 128), whole)]
        out_shape = grad_shapes + [jax.ShapeDtypeStruct((8, 128), f32)]
        scratch.append(pltpu.VMEM((3, 8, 128), f32))
    return pl.pallas_call(
        functools.partial(expert_kernel, steps=steps, own=own),
        grid_spec=pltpu.PrefetchScalarGridSpec(
            num_scalar_prefetch=1,
            grid=(steps,),
            in_specs=in_specs,
            out_specs=out_specs,
            scratch_shapes=scratch,
        ),
        out_shape=out_shape,
        compiler_params=pltpu.CompilerParams(vmem_limit_bytes=VMEM_LIMIT),
        cost_estimate=pl.CostEstimate(
            flops=(8 if own else 6) * rows * width * hidden_width,
            bytes_accessed=30 << 20,
            transcendentals=rows * hidden_width,
        ),
    )(half, *args)


def gram_kernel(info_ref, scale_ref, *refs, count):
    firsts, seconds, out_ref, acc_ref = refs[:count], refs[count : 2 * count], refs[-2], refs[-1]
    step = pl.program_id(0)
    pairs = [(j, k) for j in range(count) for k in range(j, count)]

    @pl.when(step == 0)
    def _():
        acc_ref[...] = jnp.zeros_like(acc_ref)

    for group in (firsts, seconds):
        values = [ref[...] for ref in group]
        for n, (j, k) in enumerate(pairs):
            acc_ref[n] += fold(values[j] * values[k])

    @pl.when(step == pl.num_programs(0) - 1)
    def _():
        member = info_ref[0]
        row = lax.broadcasted_iota(jnp.int32, out_ref.shape, 0)
        lane = lax.broadcasted_iota(jnp.int32, out_ref.shape, 1)
        table = jnp.where((row == member) & (lane == count), 0.5 * scale_ref[...], 0.0)
        for n, (j, k) in enumerate(pairs):
            total = jnp.sum(acc_ref[n])
            a, b = member ^ j, member ^ k
            here = ((row == a) & (lane == b)) | ((row == b) & (lane == a))
            table = jnp.where(here, total, table)
        out_ref[...] = table


def gram_call(member, scale, firsts, seconds):
    count = len(firsts)
    steps = 3
    first_block = (firsts[0].shape[0], firsts[0].shape[1] // steps)
    second_block = (seconds[0].shape[0] // steps, seconds[0].shape[1])
    rows = 8 * -(-count // 8)
    pairs = count * (count + 1) // 2
    return pl.pallas_call(
        functools.partial(gram_kernel, count=count),
        grid_spec=pltpu.PrefetchScalarGridSpec(
            num_scalar_prefetch=1,
            grid=(steps,),
            in_specs=[pl.BlockSpec((1, 1), lambda i, h: (0, 0))]
            + [pl.BlockSpec(first_block, lambda i, h: (0, i))] * count
            + [pl.BlockSpec(second_block, lambda i, h: (i, 0))] * count,
            out_specs=pl.BlockSpec((rows, 128), lambda i, h: (0, 0)),
            scratch_shapes=[pltpu.VMEM((pairs, 8, 128), f32)],
        ),
        out_shape=jax.ShapeDtypeStruct((rows, 128), f32),
        compiler_params=pltpu.CompilerParams(vmem_limit_bytes=VMEM_LIMIT),
    )(member, scale, *firsts, *seconds)


def tree_weights(table_ref, member, count):
    table = table_ref[...]
    row = lax.broadcasted_iota(jnp.int32, table.shape, 0)
    lane = lax.broadcasted_iota(jnp.int32, table.shape, 1)

    def entry(a, b):
        picked = jnp.where((row == a) & (lane == b), table, 0.0)
        return jnp.sum(jnp.sum(picked, axis=1, keepdims=True), axis=0, keepdims=True)

    unscale = [1.0 / entry(member ^ j, count) for j in range(count)]
    gram = {}
    for j in range(count):
        for k in range(j, count):
            gram[j, k] = entry(member ^ j, member ^ k) * unscale[j] * unscale[k]
    factors = {}
    left = count
    while left > 1:
        bit = left // 2
        low, high = [], []
        for j in range(bit):
            norm_low = jnp.maximum(gram[j, j], 0.0)
            norm_high = jnp.maximum(gram[j + bit, j + bit], 0.0)
            limit = jnp.sqrt(norm_low) * jnp.sqrt(norm_high)
            product = jnp.clip(gram[j, j + bit], -limit, limit)
            low.append(1.0 - product / (2.0 * (norm_low + eps_adasum)))
            high.append(1.0 - product / (2.0 * (norm_high + eps_adasum)))
        factors[bit] = (low, high)
        gram = {
            (j, k): low[j] * low[k] * gram[j, k]
            + high[j] * high[k] * gram[j + bit, k + bit]
            + (low[j] * high[k] * gram[j, k + bit] + low[k] * high[j] * gram[k, j + bit])
            for j in range(bit)
            for k in range(j, bit)
        }
        left = bit
    return unscale, factors


def update_kernel(info_ref, table_ref, *refs, count):
    firsts, seconds = refs[:count], refs[count : 2 * count]
    w1_ref, w2_ref, m1_ref, m2_ref, v1_ref, v2_ref = refs[2 * count : 2 * count + 6]
    outs = refs[2 * count + 6 :]
    unscale, factors = tree_weights(table_ref, info_ref[0], count)

    def combine(group):
        values = [group[j][...] * unscale[j] for j in range(count)]
        left = count
        while left > 1:
            left //= 2
            low, high = factors[left]
            values = [low[j] * values[j] + high[j] * values[j + left] for j in range(left)]
        return values[0]

    grad = combine(firsts)
    new = adam_update(grad, w1_ref[0].astype(f32), m1_ref[0], v1_ref[0])
    for n in range(3):
        outs[2 * n][0] = new[n]
    grad = combine(seconds).T
    new = adam_update(grad, w2_ref[0].astype(f32), m2_ref[0], v2_ref[0])
    for n in range(3):
        outs[2 * n + 1][0] = new[n]


def update_call(info, table, firsts, seconds, w1, w2, m1, m2, v1, v2):
    count = len(firsts)
    steps = 3
    rows_first, hidden_width = firsts[0].shape
    width, rows_second = seconds[0].shape
    first_block = (rows_first, hidden_width // steps)
    second_block = (width // steps, rows_second)
    first_own = pl.BlockSpec((1,) + first_block, lambda i, h: (0, 0, i))
    second_own = pl.BlockSpec((1, rows_second, width // steps), lambda i, h: (0, 0, i))
    return pl.pallas_call(
        functools.partial(update_kernel, count=count),
        grid_spec=pltpu.PrefetchScalarGridSpec(
            num_scalar_prefetch=1,
            grid=(steps,),
            in_specs=[pl.BlockSpec(table.shape, lambda i, h: (0, 0))]
            + [pl.BlockSpec(first_block, lambda i, h: (0, i))] * count
            + [pl.BlockSpec(second_block, lambda i, h: (i, 0))] * count
            + [
                pl.BlockSpec((1,) + first_block, lambda i, h: (0, h[1], i)),
                pl.BlockSpec((1, rows_second, width // steps), lambda i, h: (0, h[1], i)),
            ]
            + [first_own, second_own] * 2,
            out_specs=[first_own, second_own] * 3,
        ),
        out_shape=[
            jax.ShapeDtypeStruct((1, rows_first, hidden_width), f32),
            jax.ShapeDtypeStruct((1, rows_second, width), f32),
        ]
        * 3,
        compiler_params=pltpu.CompilerParams(vmem_limit_bytes=VMEM_LIMIT),
    )(info, table, *firsts, *seconds, w1, w2, m1, m2, v1, v2)


def body(
    tokens,
    assigned,
    gate_prob,
    cotangent,
    weight_in,
    weight_out,
    moment_in,
    moment_out,
    second_in,
    second_out,
):
    experts = lax.axis_size("expert")
    replicas = lax.axis_size("dp")
    top = replicas // 2
    self_index = lax.axis_index("dp")
    expert = lax.axis_index("expert")
    half = self_index // top
    member = self_index % top
    tok_rows, width = tokens.shape
    hidden_width = weight_in.shape[2]
    capacity = 2 * tok_rows // experts
    rows_first = width // replicas
    rows_second = hidden_width // replicas
    w_first = weight_in[0]
    w_second = weight_out[0]
    half_info = half.astype(jnp.int32).reshape(1)
    info = jnp.stack([member, self_index]).astype(jnp.int32)

    scaled = (gate_prob * cotangent.astype(f32)).astype(bf16)
    far_assigned = swap(assigned, "dp", top)
    far_tokens = swap(tokens, "dp", top)
    far_scaled = swap(scaled, "dp", top)

    table = slot_table(assigned, expert, experts, capacity)
    inputs = dispatch(table, tokens, experts)
    upstream = dispatch(table, scaled, experts)
    expert_out, own_in, own_out = expert_call(
        half_info, inputs, upstream, w_first, w_second, None
    )

    far_table = slot_table(far_assigned, expert, experts, capacity)
    far_inputs = dispatch(far_table, far_tokens, experts)
    far_upstream = dispatch(far_table, far_scaled, experts)
    far_in, far_out, mine = expert_call(
        half_info, far_inputs, far_upstream, w_first, w_second, (own_in, own_out)
    )

    theirs = swap(mine, "dp", top)
    cross = mine[0, 0] + theirs[0, 0]
    norm_own = mine[1, 0] + theirs[2, 0]
    norm_far = mine[2, 0] + theirs[1, 0]
    coef_own = 1.0 - cross / (2.0 * (norm_own + eps_adasum))
    coef_far = 1.0 - cross / (2.0 * (norm_far + eps_adasum))
    weighted = coef_own * coef_own * norm_own + coef_far * coef_far * norm_far
    norm = jnp.maximum(weighted + 2.0 * coef_own * coef_far * cross, 1e-5 * weighted)
    scale = 16384.0 * lax.rsqrt(jnp.maximum(norm, 1e-12))
    weight_own = coef_own * scale
    weight_far = coef_far * scale

    def quarter(other):
        place = member ^ other

        def part(own, far, size, axis):
            own, far = (
                lax.dynamic_slice_in_dim(x, place * size, size, axis) for x in (own, far)
            )
            return weight_own * own + weight_far * far

        return part(own_in, far_in, rows_first, 0), part(own_out, far_out, rows_second, 1)

    firsts, seconds = [], []
    for other in range(top):
        first, second = quarter(other)
        if other:
            first = swap(first.astype(f16), "dp", other).astype(f32)
            second = swap(second.astype(f16), "dp", other).astype(f32)
        firsts.append(first)
        seconds.append(second)

    products = gram_call(info, scale.reshape(1, 1), firsts, seconds)
    bit = 1
    while bit < replicas:
        products = products + swap(products, "dp", bit)
        bit *= 2
    new = update_call(
        info,
        products,
        firsts,
        seconds,
        weight_in,
        weight_out,
        moment_in,
        moment_out,
        second_in,
        second_out,
    )

    returned = exchange_blocks(
        [expert_out[j * capacity : (j + 1) * capacity] for j in range(experts)]
    )
    picked = contract_rows(table, jnp.concatenate(returned, axis=0))
    combined = (gate_prob * picked).astype(bf16)
    return (combined, *new)


def solution(mesh):
    row_spec = P(("dp", "expert"), None)
    owner_spec = P("expert", "dp", None)
    return jax.shard_map(
        body,
        mesh=mesh,
        in_specs=(row_spec,) * 4 + (P("expert", None, None),) * 2 + (owner_spec,) * 4,
        out_specs=(row_spec,) + (owner_spec,) * 6,
        check_vma=False,
    )
```

profile of v0, /device:TPU:0, one launch (start us, length us, event | category | flops | bytes accessed | tf_op | source)
XLA Modules:
  0.0 235.2 jit_solution(3901849194612769233)
XLA Ops:
  0.6 4.1 %collective-permute-start.10 = (bf16[512,768]{1,0:T(8,128)(2,1)}, bf16[512,768]{1,0:T(8,128)(2,1)}, u32[]{:S(2)}, u32[]{:S(2)}) collective-permute-start(bf16[512,768]{1,0:T(8,128)(2,1)} %param.10), channel_id=1, source_target_pairs={{0,16},{4,20},{8,24},{12,28},{16,0},{20,4},{24,8},{28,12},{1,17},{... | collective-permute-start | bytes 2359304 | tf_op jit(solution)/shard_map/ppermute | solution.py:18
  5.5 1.2 reduce-window.14
  8.6 2.2 fusion.5
  12.4 1.1 collective-permute-start.1
  15.9 23.6 %collective-permute-done.9 = s32[512,1]{0,1:T(1,128)S(1)} collective-permute-done((s32[512,1]{0,1:T(1,128)}, s32[512,1]{0,1:T(1,128)S(1)}, u32[]{:S(2)}, u32[]{:S(2)}) %collective-permute-start.9) | collective-permute-done | bytes 2080 | tf_op jit(solution)/shard_map/ppermute | solution.py:18
  40.1 1.2 reduce-window.16
  41.8 1.5 collective-permute-start.4
  44.8 6.3 %collective-permute-done.5 = bf16[256,768]{1,0:T(8,128)(2,1)} collective-permute-done((bf16[256,768]{1,0:T(8,128)(2,1)}, bf16[256,768]{1,0:T(8,128)(2,1)}, u32[]{:S(2)}, u32[]{:S(2)}) %collective-permute-start.5) | collective-permute-done | bytes 393248 | tf_op jit(solution)/shard_map/ppermute | solution.py:18
  51.2 8.4 %collective-permute-done.4 = bf16[256,768]{1,0:T(8,128)(2,1)S(1)} collective-permute-done((bf16[256,768]{1,0:T(8,128)(2,1)}, bf16[256,768]{1,0:T(8,128)(2,1)S(1)}, u32[]{:S(2)}, u32[]{:S(2)}) %collective-permute-start.4) | collective-permute-done | bytes 393248 | tf_op jit(solution)/shard_map/ppermute | solution.py:18
  60.7 2.2 fusion.7
  63.5 1.2 collective-permute-start.12
  64.9 17.5 %collective-permute-done.14 = bf16[512,768]{1,0:T(8,128)(2,1)S(1)} collective-permute-done((bf16[512,768]{1,0:T(8,128)(2,1)S(1)}, bf16[512,768]{1,0:T(8,128)(2,1)S(1)}, u32[]{:S(2)}, u32[]{:S(2)}) %collective-permute-start.14) | collective-permute-done | bytes 786464 | tf_op jit(solution)/shard_map/ppermute | solution.py:18
  83.7 1.3 collective-permute-start.16
  85.5 29.1 %shard_map.153 = (bf16[1024,768]{1,0:T(8,128)(2,1)S(1)}, f32[384,3072]{1,0:T(8,128)}, f32[768,1536]{1,0:T(8,128)}) custom-call(s32[1]{0:T(128)} %bitcast.4.half_ref, bf16[1024,768]{1,0:T(8,128)(2,1)S(1)} %pad_maximum_fusion.x_ref, bf16[1024,768]{1,0:T(8,128)(2,1)S(1)} %pad_maximum_fusion.1.u_ref, bf16[768,3072]{1,0:T(8,128)(2,1)} %bitcast.56, ...), custom_call_target="tpu_custom_call" | custom-call | flops 19327352832 | bytes 31457280 | tf_op jit(solution)/shard_map/pallas_call | solution.py:186
  114.8 25.0 %shard_map.154 = (f32[384,3072]{1,0:T(8,128)}, f32[768,1536]{1,0:T(8,128)}, f32[8,128]{1,0:T(8,128)S(1)}) custom-call(s32[1]{0:T(128)} %bitcast.4.half_ref, bf16[1024,768]{1,0:T(8,128)(2,1)S(1)} %pad_maximum_fusion.2.x_ref, bf16[1024,768]{1,0:T(8,128)(2,1)S(1)} %pad_maximum_fusion.3.u_ref, bf16[768,3072]{1,0:T(8,128)(2,1)} %bitcast.57, ...), custom_call_target="tpu_custom_call" | custom-call | flops 14495514624 | bytes 31457280 | tf_op jit(solution)/shard_map/pallas_call | solution.py:186
  140.3 4.0 %collective-permute-done.18 = f32[8,128]{1,0:T(8,128)S(1)} collective-permute-done((f32[8,128]{1,0:T(8,128)S(1)}, f32[8,128]{1,0:T(8,128)S(1)}, u32[]{:S(2)}, u32[]{:S(2)}) %collective-permute-start.18) | collective-permute-done | bytes 4128 | tf_op jit(solution)/shard_map/ppermute | solution.py:18
  149.0 5.6 %add_convert_fusion.3 = (f16[96,3072]{1,0:T(8,128)(2,1)}, f16[96,3072]{1,0:T(8,128)(2,1)}, f16[96,3072]{1,0:T(8,128)(2,1)}, f32[96,3072]{1,0:T(8,128)S(1)}) fusion(f32[384,3072]{1,0:T(8,128)} %get-tuple-element.23, s32[]{:T(128)S(6)} %select_n.48, f32[384,3072]{1,0:T(8,128)} %get-tuple-element.20.rest_0_, f32[]{:T(128)S(6)} %mul.194, f32[]{:T(128)S(6)} %mul.190, ...), kind=kLoop, calls=%fused_computation.28 | loop fusion | flops 4423680 | bytes 12386328 | tf_op jit(solution)/shard_map/convert_element_type | solution.py:427
  154.6 1.5 collective-permute-start.19
  156.1 2.0 collective-permute-start.21
  158.1 4.4 %add_convert_fusion = (f16[768,384]{1,0:T(8,128)(2,1)S(1)}, f16[768,384]{1,0:T(8,128)(2,1)S(1)}, f16[768,384]{1,0:T(8,128)(2,1)S(1)}, f32[768,384]{1,0:T(8,128)S(1)}) fusion(f32[768,1536]{1,0:T(8,128)} %get-tuple-element.24, s32[]{:T(128)S(6)} %select_n.52, f32[768,1536]{1,0:T(8,128)} %get-tuple-element.21.rest_1_, f32[]{:T(128)S(6)} %mul.194, f32[]{:T(128)S(6)} %mul.190, ...), kind=kLoop, calls=%fused_computation.24 | loop fusion | flops 4423680 | bytes 12386328 | tf_op jit(solution)/shard_map/convert_element_type | solution.py:428
  162.5 1.6 collective-permute-start.22
  164.1 18.1 %collective-permute-done.19 = f16[96,3072]{1,0:T(8,128)(2,1)S(1)} collective-permute-done((f16[96,3072]{1,0:T(8,128)(2,1)}, f16[96,3072]{1,0:T(8,128)(2,1)S(1)}, u32[]{:S(2)}, u32[]{:S(2)}) %collective-permute-start.19) | collective-permute-done | bytes 589856 | tf_op jit(solution)/shard_map/ppermute | solution.py:18
  182.4 2.8 %collective-permute-done.21 = f16[96,3072]{1,0:T(8,128)(2,1)S(1)} collective-permute-done((f16[96,3072]{1,0:T(8,128)(2,1)}, f16[96,3072]{1,0:T(8,128)(2,1)S(1)}, u32[]{:S(2)}, u32[]{:S(2)}) %collective-permute-start.21) | collective-permute-done | bytes 589856 | tf_op jit(solution)/shard_map/ppermute | solution.py:18
  186.0 9.4 %collective-permute-done.22 = f16[768,384]{1,0:T(8,128)(2,1)S(1)} collective-permute-done((f16[768,384]{1,0:T(8,128)(2,1)S(1)}, f16[768,384]{1,0:T(8,128)(2,1)S(1)}, u32[]{:S(2)}, u32[]{:S(2)}) %collective-permute-start.22) | collective-permute-done | bytes 589856 | tf_op jit(solution)/shard_map/ppermute | solution.py:18
  199.0 9.0 %collective-permute-done.24 = f16[768,384]{1,0:T(8,128)(2,1)S(1)} collective-permute-done((f16[768,384]{1,0:T(8,128)(2,1)S(1)}, f16[768,384]{1,0:T(8,128)(2,1)S(1)}, u32[]{:S(2)}, u32[]{:S(2)}) %collective-permute-start.24) | collective-permute-done | bytes 589856 | tf_op jit(solution)/shard_map/ppermute | solution.py:18
  209.2 5.0 %shard_map.155 = f32[8,128]{1,0:T(8,128)S(1)} custom-call(s32[2]{0:T(128)S(1)} %pad_add_fusion.info_ref, f32[1,1]{1,0:T(1,128)} %bitcast.15.scale_ref, f32[96,3072]{1,0:T(8,128)S(1)} %get-tuple-element.38.refs_0_, f32[96,3072]{1,0:T(8,128)S(1)} %convert_element_type.85.refs_1_, f32[96,3072]{1,0:T(8,128)S(1)} %convert_element_type.87.refs_2_, ...), custom_call_target="tpu_custom_call" | custom-call | tf_op jit(solution)/shard_map/pallas_call | solution.py:240
  214.2 1.6 collective-permute-start.25
  215.8 2.1 collective-permute-done.25
  218.1 3.3 %collective-permute-done.26 = f32[8,128]{1,0:T(8,128)S(1)} collective-permute-done((f32[8,128]{1,0:T(8,128)S(1)}, f32[8,128]{1,0:T(8,128)S(1)}, u32[]{:S(2)}, u32[]{:S(2)}) %collective-permute-start.26) | collective-permute-done | bytes 4128 | tf_op jit(solution)/shard_map/ppermute | solution.py:18
  221.8 2.1 multiply_convert_fusion
  224.0 2.0 collective-permute-done.27
  226.0 9.1 %shard_map.156 = (f32[1,96,3072]{2,1,0:T(8,128)}, f32[1,384,768]{2,1,0:T(8,128)}, f32[1,96,3072]{2,1,0:T(8,128)}, f32[1,384,768]{2,1,0:T(8,128)}, f32[1,96,3072]{2,1,0:T(8,128)}, /*index=5*/f32[1,384,768]{2,1,0:T(8,128)}) custom-call(s32[2]{0:T(128)S(1)} %pad_add_fusion.info_ref, f32[8,128]{1,0:T(8,128)S(1)} %add.145.table_ref, ...), custom_call_target="tpu_custom_call" | custom-call | tf_op jit(solution)/shard_map/pallas_call | solution.py:328
  (83 shorter events, 20.5 us)
Async XLA Ops:
  0.6 60.0 %collective-permute-start.10 = (bf16[512,768]{1,0:T(8,128)(2,1)}, bf16[512,768]{1,0:T(8,128)(2,1)}, u32[]{:S(2)}, u32[]{:S(2)}) collective-permute-start(bf16[512,768]{1,0:T(8,128)(2,1)} %param.10), channel_id=1, source_target_pairs={{0,16},{4,20},{8,24},{12,28},{16,0},{20,4},{24,8},{28,12},{1,17},{... | collective-permute-start | bytes 2359304 | tf_op jit(solution)/shard_map/ppermute | solution.py:18
  4.7 34.8 %collective-permute-start.9 = (s32[512,1]{0,1:T(1,128)}, s32[512,1]{0,1:T(1,128)S(1)}, u32[]{:S(2)}, u32[]{:S(2)}) collective-permute-start(s32[512,1]{0,1:T(1,128)} %param.11), channel_id=1, source_target_pairs={{0,16},{4,20},{8,24},{12,28},{16,0},{20,4},{24,8},{28,12},{1,17},{... | collective-permute-start | bytes 6152 | tf_op jit(solution)/shard_map/ppermute | solution.py:18
  8.6 5.3 %copy-start.4 = (s32[512]{0:T(512)}, s32[512]{0:T(512)S(1)}, u32[]{:S(2)}) copy-start(s32[512]{0:T(512)S(1)} %multiply_add_fusion.3) | copy-start | bytes 6148
  10.8 2.9 %copy-start = (bf16[512,768]{1,0:T(8,128)(2,1)S(1)}, bf16[512,768]{1,0:T(8,128)(2,1)}, u32[]{:S(2)}) copy-start(bf16[512,768]{1,0:T(8,128)(2,1)} %param.13) | copy-start | bytes 2359300
  11.8 30.0 %collective-permute-start.2 = (bf16[256,768]{1,0:T(8,128)(2,1)}, bf16[256,768]{1,0:T(8,128)(2,1)S(1)}, u32[]{:S(2)}, u32[]{:S(2)}) collective-permute-start(bf16[256,768]{1,0:T(8,128)(2,1)} %get-tuple-element.56), channel_id=1, source_target_pairs={{0,3},{1,2},{2,1},{3,0},{4,7},{5,6},{6,5},{7,4},{8,11},{9,10},{10,... | collective-permute-start | bytes 1179656 | tf_op jit(solution)/shard_map/ppermute | solution.py:18
  12.4 30.9 %collective-permute-start.1 = (bf16[256,768]{1,0:T(8,128)(2,1)}, bf16[256,768]{1,0:T(8,128)(2,1)S(1)}, u32[]{:S(2)}, u32[]{:S(2)}) collective-permute-start(bf16[256,768]{1,0:T(8,128)(2,1)} %get-tuple-element.57), channel_id=1, source_target_pairs={{0,2},{1,3},{2,0},{3,1},{4,6},{5,7},{6,4},{7,5},{8,10},{9,11},{10,... | collective-permute-start | bytes 1179656 | tf_op jit(solution)/shard_map/ppermute | solution.py:18
  13.6 31.1 %collective-permute-start = (bf16[256,768]{1,0:T(8,128)(2,1)S(1)}, bf16[256,768]{1,0:T(8,128)(2,1)S(1)}, u32[]{:S(2)}, u32[]{:S(2)}) collective-permute-start(bf16[256,768]{1,0:T(8,128)(2,1)S(1)} %get-tuple-element.58), channel_id=1, source_target_pairs={{0,1},{1,0},{2,3},{3,2},{4,5},{5,4},{6,7},{7,6},{8,9},{9,8},{10,11... | collective-permute-start | bytes 1179656 | tf_op jit(solution)/shard_map/ppermute | solution.py:18
  39.5 11.6 %collective-permute-start.5 = (bf16[256,768]{1,0:T(8,128)(2,1)}, bf16[256,768]{1,0:T(8,128)(2,1)}, u32[]{:S(2)}, u32[]{:S(2)}) collective-permute-start(bf16[256,768]{1,0:T(8,128)(2,1)} %get-tuple-element.52), channel_id=1, source_target_pairs={{0,3},{1,2},{2,1},{3,0},{4,7},{5,6},{6,5},{7,4},{8,11},{9,10},{10,... | collective-permute-start | bytes 1179656 | tf_op jit(solution)/shard_map/ppermute | solution.py:18
  41.8 17.8 %collective-permute-start.4 = (bf16[256,768]{1,0:T(8,128)(2,1)}, bf16[256,768]{1,0:T(8,128)(2,1)S(1)}, u32[]{:S(2)}, u32[]{:S(2)}) collective-permute-start(bf16[256,768]{1,0:T(8,128)(2,1)} %get-tuple-element.53), channel_id=1, source_target_pairs={{0,2},{1,3},{2,0},{3,1},{4,6},{5,7},{6,4},{7,5},{8,10},{9,11},{10,... | collective-permute-start | bytes 1179656 | tf_op jit(solution)/shard_map/ppermute | solution.py:18
  43.3 16.2 %collective-permute-start.3 = (bf16[256,768]{1,0:T(8,128)(2,1)S(1)}, bf16[256,768]{1,0:T(8,128)(2,1)S(1)}, u32[]{:S(2)}, u32[]{:S(2)}) collective-permute-start(bf16[256,768]{1,0:T(8,128)(2,1)S(1)} %get-tuple-element.54), channel_id=1, source_target_pairs={{0,1},{1,0},{2,3},{3,2},{4,5},{5,4},{6,7},{7,6},{8,9},{9,8},{10,11... | collective-permute-start | bytes 1179656 | tf_op jit(solution)/shard_map/ppermute | solution.py:18
  44.7 37.7 %collective-permute-start.14 = (bf16[512,768]{1,0:T(8,128)(2,1)S(1)}, bf16[512,768]{1,0:T(8,128)(2,1)S(1)}, u32[]{:S(2)}, u32[]{:S(2)}) collective-permute-start(bf16[512,768]{1,0:T(8,128)(2,1)S(1)} %multiply_convert_fusion.1), channel_id=1, source_target_pairs={{0,16},{4,20},{8,24},{12,28},{16,0},{20,4},{24,8},{28,12},{1,17},{... | collective-permute-start | bytes 2359304 | tf_op jit(solution)/shard_map/ppermute | solution.py:18
  63.0 22.0 %collective-permute-start.13 = (bf16[256,768]{1,0:T(8,128)(2,1)S(1)}, bf16[256,768]{1,0:T(8,128)(2,1)S(1)}, u32[]{:S(2)}, u32[]{:S(2)}) collective-permute-start(bf16[256,768]{1,0:T(8,128)(2,1)S(1)} %get-tuple-element.44), channel_id=1, source_target_pairs={{0,3},{1,2},{2,1},{3,0},{4,7},{5,6},{6,5},{7,4},{8,11},{9,10},{10,... | collective-permute-start | bytes 1179656 | tf_op jit(solution)/shard_map/ppermute | solution.py:18
  63.5 51.1 %collective-permute-start.12 = (bf16[256,768]{1,0:T(8,128)(2,1)S(1)}, bf16[256,768]{1,0:T(8,128)(2,1)S(1)}, u32[]{:S(2)}, u32[]{:S(2)}) collective-permute-start(bf16[256,768]{1,0:T(8,128)(2,1)S(1)} %get-tuple-element.45), channel_id=1, source_target_pairs={{0,2},{1,3},{2,0},{3,1},{4,6},{5,7},{6,4},{7,5},{8,10},{9,11},{10,... | collective-permute-start | bytes 1179656 | tf_op jit(solution)/shard_map/ppermute | solution.py:18
  64.7 49.9 %collective-permute-start.11 = (bf16[256,768]{1,0:T(8,128)(2,1)S(1)}, bf16[256,768]{1,0:T(8,128)(2,1)S(1)}, u32[]{:S(2)}, u32[]{:S(2)}) collective-permute-start(bf16[256,768]{1,0:T(8,128)(2,1)S(1)} %get-tuple-element.46), channel_id=1, source_target_pairs={{0,1},{1,0},{2,3},{3,2},{4,5},{5,4},{6,7},{7,6},{8,9},{9,8},{10,11... | collective-permute-start | bytes 1179656 | tf_op jit(solution)/shard_map/ppermute | solution.py:18
  83.6 31.1 %collective-permute-start.17 = (bf16[256,768]{1,0:T(8,128)(2,1)S(1)}, bf16[256,768]{1,0:T(8,128)(2,1)S(1)}, u32[]{:S(2)}, u32[]{:S(2)}) collective-permute-start(bf16[256,768]{1,0:T(8,128)(2,1)S(1)} %get-tuple-element.40), channel_id=1, source_target_pairs={{0,3},{1,2},{2,1},{3,0},{4,7},{5,6},{6,5},{7,4},{8,11},{9,10},{10,... | collective-permute-start | bytes 1179656 | tf_op jit(solution)/shard_map/ppermute | solution.py:18
  83.7 31.1 %collective-permute-start.16 = (bf16[256,768]{1,0:T(8,128)(2,1)S(1)}, bf16[256,768]{1,0:T(8,128)(2,1)S(1)}, u32[]{:S(2)}, u32[]{:S(2)}) collective-permute-start(bf16[256,768]{1,0:T(8,128)(2,1)S(1)} %get-tuple-element.41), channel_id=1, source_target_pairs={{0,2},{1,3},{2,0},{3,1},{4,6},{5,7},{6,4},{7,5},{8,10},{9,11},{10,... | collective-permute-start | bytes 1179656 | tf_op jit(solution)/shard_map/ppermute | solution.py:18
  85.0 29.7 %collective-permute-start.15 = (bf16[256,768]{1,0:T(8,128)(2,1)S(1)}, bf16[256,768]{1,0:T(8,128)(2,1)S(1)}, u32[]{:S(2)}, u32[]{:S(2)}) collective-permute-start(bf16[256,768]{1,0:T(8,128)(2,1)S(1)} %get-tuple-element.42), channel_id=1, source_target_pairs={{0,1},{1,0},{2,3},{3,2},{4,5},{5,4},{6,7},{7,6},{8,9},{9,8},{10,11... | collective-permute-start | bytes 1179656 | tf_op jit(solution)/shard_map/ppermute | solution.py:18
  139.8 4.5 %collective-permute-start.18 = (f32[8,128]{1,0:T(8,128)S(1)}, f32[8,128]{1,0:T(8,128)S(1)}, u32[]{:S(2)}, u32[]{:S(2)}) collective-permute-start(f32[8,128]{1,0:T(8,128)S(1)} %get-tuple-element.22), channel_id=1, source_target_pairs={{0,16},{4,20},{8,24},{12,28},{16,0},{20,4},{24,8},{28,12},{1,17},{... | collective-permute-start | bytes 12296 | tf_op jit(solution)/shard_map/ppermute | solution.py:18
  154.6 27.6 %collective-permute-start.19 = (f16[96,3072]{1,0:T(8,128)(2,1)}, f16[96,3072]{1,0:T(8,128)(2,1)S(1)}, u32[]{:S(2)}, u32[]{:S(2)}) collective-permute-start(f16[96,3072]{1,0:T(8,128)(2,1)} %get-tuple-element.37), channel_id=1, source_target_pairs={{0,4},{4,0},{8,12},{12,8},{16,20},{20,16},{24,28},{28,24},{1,5},{5... | collective-permute-start | bytes 1769480 | tf_op jit(solution)/shard_map/ppermute | solution.py:18
  156.1 26.2 %collective-permute-start.20 = (f16[96,3072]{1,0:T(8,128)(2,1)}, f16[96,3072]{1,0:T(8,128)(2,1)S(1)}, u32[]{:S(2)}, u32[]{:S(2)}) collective-permute-start(f16[96,3072]{1,0:T(8,128)(2,1)} %get-tuple-element.36), channel_id=1, source_target_pairs={{0,8},{4,12},{8,0},{12,4},{16,24},{20,28},{24,16},{28,20},{1,9},{5... | collective-permute-start | bytes 1769480 | tf_op jit(solution)/shard_map/ppermute | solution.py:18
  156.1 29.1 %collective-permute-start.21 = (f16[96,3072]{1,0:T(8,128)(2,1)}, f16[96,3072]{1,0:T(8,128)(2,1)S(1)}, u32[]{:S(2)}, u32[]{:S(2)}) collective-permute-start(f16[96,3072]{1,0:T(8,128)(2,1)} %get-tuple-element.35), channel_id=1, source_target_pairs={{0,12},{4,8},{8,4},{12,0},{16,28},{20,24},{24,20},{28,16},{1,13},{... | collective-permute-start | bytes 1769480 | tf_op jit(solution)/shard_map/ppermute | solution.py:18
  162.5 32.9 %collective-permute-start.22 = (f16[768,384]{1,0:T(8,128)(2,1)S(1)}, f16[768,384]{1,0:T(8,128)(2,1)S(1)}, u32[]{:S(2)}, u32[]{:S(2)}) collective-permute-start(f16[768,384]{1,0:T(8,128)(2,1)S(1)} %get-tuple-element.33), channel_id=1, source_target_pairs={{0,4},{4,0},{8,12},{12,8},{16,20},{20,16},{24,28},{28,24},{1,5},{5... | collective-permute-start | bytes 1769480 | tf_op jit(solution)/shard_map/ppermute | solution.py:18
  164.1 33.8 %collective-permute-start.23 = (f16[768,384]{1,0:T(8,128)(2,1)S(1)}, f16[768,384]{1,0:T(8,128)(2,1)S(1)}, u32[]{:S(2)}, u32[]{:S(2)}) collective-permute-start(f16[768,384]{1,0:T(8,128)(2,1)S(1)} %get-tuple-element.32), channel_id=1, source_target_pairs={{0,8},{4,12},{8,0},{12,4},{16,24},{20,28},{24,16},{28,20},{1,9},{5... | collective-permute-start | bytes 1769480 | tf_op jit(solution)/shard_map/ppermute | solution.py:18
  182.2 25.9 %collective-permute-start.24 = (f16[768,384]{1,0:T(8,128)(2,1)S(1)}, f16[768,384]{1,0:T(8,128)(2,1)S(1)}, u32[]{:S(2)}, u32[]{:S(2)}) collective-permute-start(f16[768,384]{1,0:T(8,128)(2,1)S(1)} %get-tuple-element.31), channel_id=1, source_target_pairs={{0,12},{4,8},{8,4},{12,0},{16,28},{20,24},{24,20},{28,16},{1,13},{... | collective-permute-start | bytes 1769480 | tf_op jit(solution)/shard_map/ppermute | solution.py:18
  182.3 39.5 %collective-permute-start.8 = (bf16[256,768]{1,0:T(8,128)(2,1)S(1)}, bf16[256,768]{1,0:T(8,128)(2,1)S(1)}, u32[]{:S(2)}, u32[]{:S(2)}) collective-permute-start(bf16[256,768]{1,0:T(8,128)(2,1)S(1)} %get-tuple-element.48), channel_id=1, source_target_pairs={{0,3},{1,2},{2,1},{3,0},{4,7},{5,6},{6,5},{7,4},{8,11},{9,10},{10,... | collective-permute-start | bytes 1179656 | tf_op jit(solution)/shard_map/ppermute | solution.py:18
  185.2 36.6 %collective-permute-start.7 = (bf16[256,768]{1,0:T(8,128)(2,1)S(1)}, bf16[256,768]{1,0:T(8,128)(2,1)S(1)}, u32[]{:S(2)}, u32[]{:S(2)}) collective-permute-start(bf16[256,768]{1,0:T(8,128)(2,1)S(1)} %get-tuple-element.49), channel_id=1, source_target_pairs={{0,2},{1,3},{2,0},{3,1},{4,6},{5,7},{6,4},{7,5},{8,10},{9,11},{10,... | collective-permute-start | bytes 1179656 | tf_op jit(solution)/shard_map/ppermute | solution.py:18
  195.4 26.4 %collective-permute-start.6 = (bf16[256,768]{1,0:T(8,128)(2,1)S(1)}, bf16[256,768]{1,0:T(8,128)(2,1)S(1)}, u32[]{:S(2)}, u32[]{:S(2)}) collective-permute-start(bf16[256,768]{1,0:T(8,128)(2,1)S(1)} %get-tuple-element.50), channel_id=1, source_target_pairs={{0,1},{1,0},{2,3},{3,2},{4,5},{5,4},{6,7},{7,6},{8,9},{9,8},{10,11... | collective-permute-start | bytes 1179656 | tf_op jit(solution)/shard_map/ppermute | solution.py:18
  209.2 12.6 %copy-start.3 = (f32[512,1]{0,1:T(1,128)S(1)}, f32[512,1]{0,1:T(1,128)}, u32[]{:S(2)}) copy-start(f32[512,1]{0,1:T(1,128)} %param.12) | copy-start | bytes 6148
  209.2 12.6 %copy-start.5 = (s32[512]{0:T(512)S(1)}, s32[512]{0:T(512)}, u32[]{:S(2)}) copy-start(s32[512]{0:T(512)} %copy-done.4) | copy-start | bytes 6148
  214.2 3.7 %collective-permute-start.25 = (f32[8,128]{1,0:T(8,128)S(1)}, f32[8,128]{1,0:T(8,128)S(1)}, u32[]{:S(2)}, u32[]{:S(2)}) collective-permute-start(f32[8,128]{1,0:T(8,128)S(1)} %shard_map.155), channel_id=1, source_target_pairs={{0,4},{4,0},{8,12},{12,8},{16,20},{20,16},{24,28},{28,24},{1,5},{5... | collective-permute-start | bytes 12296 | tf_op jit(solution)/shard_map/ppermute | solution.py:18
  217.9 3.6 %collective-permute-start.26 = (f32[8,128]{1,0:T(8,128)S(1)}, f32[8,128]{1,0:T(8,128)S(1)}, u32[]{:S(2)}, u32[]{:S(2)}) collective-permute-start(f32[8,128]{1,0:T(8,128)S(1)} %add.143), channel_id=1, source_target_pairs={{0,8},{4,12},{8,0},{12,4},{16,24},{20,28},{24,16},{28,20},{1,9},{5... | collective-permute-start | bytes 12296 | tf_op jit(solution)/shard_map/ppermute | solution.py:18
  221.5 4.5 %collective-permute-start.27 = (f32[8,128]{1,0:T(8,128)S(1)}, f32[8,128]{1,0:T(8,128)S(1)}, u32[]{:S(2)}, u32[]{:S(2)}) collective-permute-start(f32[8,128]{1,0:T(8,128)S(1)} %add.144), channel_id=1, source_target_pairs={{0,16},{4,20},{8,24},{12,28},{16,0},{20,4},{24,8},{28,12},{1,17},{... | collective-permute-start | bytes 12296 | tf_op jit(solution)/shard_map/ppermute | solution.py:18
  (2 other events, 3.5 us)
where the time goes:
time: 236 us; the launch traced here: 235 us
  waiting for transfers between devices  108 us (46%)
  Pallas kernels  68.1 us (29%)
  other arithmetic  21.8 us (9%)
  starting transfers between devices  19.8 us (8%)
  matrix products  8.49 us (4%)
  between operations  5.13 us (2%)
  local copies, waits for them, and re-layouts  4.27 us (2%)
    ppermute x28, waiting for transfers between devices, swap(): lax.ppermute(x, axis, [(i, i ^ offset) for i in range(lax.axis_size(axis))])  108 us
    pallas_call x2, Pallas kernels, expert_call(): pl.pallas_call(functools.partial(expert_kernel, steps=steps, own=own), gr...  54 us
    ppermute x28, starting transfers between devices, swap(): lax.ppermute(x, axis, [(i, i ^ offset) for i in range(lax.axis_size(axis))])  19.8 us
    pallas_call x1, Pallas kernels, update_call(): pl.pallas_call(functools.partial(update_kernel, count=count), grid_spec=p...  9.07 us
    convert_element_type x4, other arithmetic, body(): second = swap(second.astype(f16), 'dp', other).astype(f32)  7.75 us
    dot_general x4, matrix products, dispatch(): sent = jnp.dot(table, rows, preferred_element_type=f32).astype(bf16)  6.37 us
    convert_element_type x4, other arithmetic, body(): first = swap(first.astype(f16), 'dp', other).astype(f32)  5.89 us
    pallas_call x1, Pallas kernels, gram_call(): pl.pallas_call(functools.partial(gram_kernel, count=count), grid_spec=plt...  4.96 us
  transfers between devices with their start and end apart: 28, of which 13 were waited for; matrix products, arithmetic and copies ran while one was open for 12% of the time, Pallas kernels for 14%

commit v1 on v0

v1 whole, which is shorter than its diff:
```python
import functools

import jax
import jax.numpy as jnp
from jax import lax
from jax.experimental import pallas as pl
from jax.experimental.pallas import tpu as pltpu
from jax.sharding import PartitionSpec as P

eps_adasum = 1e-06
f32 = jnp.float32
bf16 = jnp.bfloat16
f16 = jnp.float16
VMEM_LIMIT = 48 << 20
GRAM_LIMIT = 8 << 20
UPDATE_LIMIT = 20 << 20
COST = 1 << 10
COST = 1 << 10
TOKEN_PIECES = 1
SCALED_PIECES = 1
CHAIN = False


def swap(x, axis, offset):
    return lax.ppermute(x, axis, [(i, i ^ offset) for i in range(lax.axis_size(axis))])


def gelu_and_slope(values):
    root = 0.7978845608028654
    square = values * values
    tanh = jnp.tanh(values * (root + (root * 0.044715) * square))
    cdf = 0.5 + 0.5 * tanh
    slope = cdf + (0.5 * values) * (1.0 - tanh * tanh) * (root + (3.0 * root * 0.044715) * square)
    return values * cdf, slope


def adam_update(grad, weight, moment, second):
    new_moment = 0.9 * moment + 0.1 * grad
    new_second = 0.999 * second + 0.001 * grad * grad
    corr_one = 1.0 - 0.9**10.0
    corr_two = 1.0 - 0.999**10.0
    update = new_moment / corr_one / (jnp.sqrt(new_second / corr_two) + 1e-08)
    return (weight - 0.001 * update, new_moment, new_second)


def contract_rows(left, right):
    return lax.dot_general(
        left, right, (((0,), (0,)), ((), ())), preferred_element_type=f32
    )


def slot_table(assigned, expert, experts, capacity):
    expert_ids = assigned[:, 0]
    one_hot = (expert_ids[:, None] == jnp.arange(experts, dtype=jnp.int32)[None, :]).astype(
        jnp.int32
    )
    slot_index = jnp.sum((jnp.cumsum(one_hot, axis=0) - one_hot) * one_hot, axis=1)
    slot_code = (expert_ids ^ expert) * capacity + slot_index
    rows = experts * capacity
    return (jnp.arange(rows, dtype=jnp.int32)[:, None] == slot_code[None, :]).astype(bf16)


def exchange_blocks(blocks):
    return [blocks[0]] + [swap(blocks[j], "expert", j) for j in range(1, len(blocks))]


def place_rows(table, rows, experts):
    capacity = table.shape[0] // experts
    sent = jnp.dot(table, rows, preferred_element_type=f32).astype(bf16)
    return [sent[j * capacity : (j + 1) * capacity] for j in range(experts)]


def dispatch(table, rows, experts):
    placed = place_rows(table, rows, experts)
    return jnp.concatenate(exchange_blocks(placed), axis=0), placed


def fold(values):
    rows = values.reshape(values.shape[0] // 8, 8, values.shape[1]).sum(0)
    spare = -rows.shape[1] % 128
    if spare:
        rows = jnp.concatenate([rows, jnp.zeros((8, spare), f32)], axis=1)
    return sum(rows[:, k * 128 : (k + 1) * 128] for k in range(rows.shape[1] // 128))


def expert_kernel(info_ref, x_ref, u_ref, w1_ref, w2_ref, *rest, steps, kind):
    if kind == "first":
        gi_ref, go_ref, sum_ref, xt_ref, ut_ref = rest
    elif kind == "second":
        before_ref, _, gi_ref, out_ref, xt_ref, sum_ref = rest
    else:
        own_gi_ref, own_go_ref, gi_ref, go_ref, stat_ref, xt_ref, ut_ref, acc_ref = rest
    step = pl.program_id(0)
    half_width = xt_ref.shape[0]

    @pl.when(step == 0)
    def _():
        start = pl.multiple_of(info_ref[2] * half_width, half_width)
        xt_ref[...] = x_ref[:, pl.ds(start, half_width)].T
        if kind != "second":
            ut_ref[...] = u_ref[...].T

    pre = jnp.dot(x_ref[...], w1_ref[...], preferred_element_type=f32)
    back = lax.dot_general(
        u_ref[...], w2_ref[...], (((1,), (1,)), ((), ())), preferred_element_type=f32
    )
    act, slope = gelu_and_slope(pre)
    hidden = act.astype(bf16)
    hidden_grad = (slope * back).astype(bf16)
    gi_ref[...] = jnp.dot(xt_ref[...], hidden_grad, preferred_element_type=f32)

    if kind == "first":
        go_ref[...] = jnp.dot(ut_ref[...], hidden, preferred_element_type=f32)
    elif kind == "far":

        @pl.when(step < steps // 2)
        def _():
            go_ref[...] = jnp.dot(ut_ref[...], hidden, preferred_element_type=f32)

    if kind == "far":

        def add(mine, far):
            acc_ref[0] += fold(mine * far)
            acc_ref[1] += fold(mine * mine)
            acc_ref[2] += fold(far * far)

        @pl.when(step == 0)
        def _():
            acc_ref[...] = jnp.zeros_like(acc_ref)

        add(own_gi_ref[...], gi_ref[...])

        @pl.when(step < steps // 2)
        def _():
            add(own_go_ref[...], go_ref[...])

        @pl.when(step == steps - 1)
        def _():
            row = lax.broadcasted_iota(jnp.int32, (8, 128), 0)
            stats = jnp.zeros((8, 128), f32)
            for k in range(3):
                stats = jnp.where(row == k, jnp.sum(acc_ref[k]), stats)
            stat_ref[...] = stats

    else:
        product = jnp.dot(hidden, w2_ref[...], preferred_element_type=f32)

        @pl.when(step == 0)
        def _():
            sum_ref[...] = product if kind == "first" else before_ref[...] + product

        @pl.when(step > 0)
        def _():
            sum_ref[...] += product

        if kind == "second":

            @pl.when(step == steps // 2 - 1)
            def _():
                out_ref[...] = sum_ref[...].astype(bf16)


def expert_call(kind, info, x, u, w1, w2, *previous):
    rows, width = x.shape
    hidden_width = w1.shape[1]
    steps = 6
    block = hidden_width // steps
    shift = steps // 2 if kind == "second" else 0

    def column(i, h):
        return (0, (i + shift + h[2] * (steps // 2)) % steps)

    def row(i, h):
        return ((i + shift + h[2] * (steps // 2)) % steps, 0)

    def held(i, h):
        return (0, jnp.minimum(i, steps // 2 - 1))

    def whole(i, h):
        return (0, 0)

    one = pl.Buffered(1)
    whole_spec = pl.BlockSpec((rows, width), whole, pipeline_mode=one)
    in_specs = [
        whole_spec,
        whole_spec,
        pl.BlockSpec((width, block), column),
        pl.BlockSpec((block, width), row),
    ]
    gi_spec = pl.BlockSpec((width // 2, block), column)
    go_spec = pl.BlockSpec((width, block), held)
    gi_shape = jax.ShapeDtypeStruct((width // 2, hidden_width), f32)
    go_shape = jax.ShapeDtypeStruct((width, hidden_width // 2), f32)
    sum_shape = jax.ShapeDtypeStruct((rows, width), f32)
    xt = pltpu.VMEM((width // 2, rows), bf16)
    ut = pltpu.VMEM((width, rows), bf16)
    aliases = {}
    if kind == "first":
        out_specs = [gi_spec, go_spec, whole_spec]
        out_shape = [gi_shape, go_shape, sum_shape]
        scratch = [xt, ut]
    elif kind == "second":
        in_specs += [whole_spec, pl.BlockSpec(memory_space=pl.ANY)]
        out_specs = [gi_spec, whole_spec]
        out_shape = [gi_shape, jax.ShapeDtypeStruct((rows, width), bf16)]
        scratch = [xt, pltpu.VMEM((rows, width), f32)]
        aliases = {6: 0}
    else:
        in_specs += [gi_spec, go_spec]
        out_specs = [gi_spec, go_spec, pl.BlockSpec((8, 128), whole)]
        out_shape = [gi_shape, go_shape, jax.ShapeDtypeStruct((8, 128), f32)]
        scratch = [xt, ut, pltpu.VMEM((3, 8, 128), f32)]
    return pl.pallas_call(
        functools.partial(expert_kernel, steps=steps, kind=kind),
        grid_spec=pltpu.PrefetchScalarGridSpec(
            num_scalar_prefetch=1,
            grid=(steps if kind == "far" else steps // 2,),
            in_specs=in_specs,
            out_specs=out_specs,
            scratch_shapes=scratch,
        ),
        out_shape=out_shape,
        input_output_aliases=aliases,
        compiler_params=pltpu.CompilerParams(vmem_limit_bytes=VMEM_LIMIT),
        cost_estimate=pl.CostEstimate(
            flops=COST, bytes_accessed=COST, transcendentals=0
        ),
    )(info, x, u, w1, w2, *previous)


def gram_kernel(info_ref, before_ref, *refs, count, opening):
    group, out_ref, acc_ref = refs[:count], refs[-2], refs[-1]
    step = pl.program_id(0)
    pairs = [(j, k) for j in range(count) for k in range(j, count)]

    @pl.when(step == 0)
    def _():
        acc_ref[...] = jnp.zeros_like(acc_ref)

    values = [ref[...] for ref in group]
    for n, (j, k) in enumerate(pairs):
        acc_ref[n] += fold(values[j] * values[k])

    @pl.when(step == pl.num_programs(0) - 1)
    def _():
        member = info_ref[0]
        row = lax.broadcasted_iota(jnp.int32, out_ref.shape, 0)
        lane = lax.broadcasted_iota(jnp.int32, out_ref.shape, 1)
        table = jnp.zeros(out_ref.shape, f32)
        if opening:
            table = jnp.where((row == member) & (lane == count), 0.5 * before_ref[...], 0.0)
        for n, (j, k) in enumerate(pairs):
            total = jnp.sum(acc_ref[n])
            a, b = member ^ j, member ^ k
            here = ((row == a) & (lane == b)) | ((row == b) & (lane == a))
            table = jnp.where(here, total, table)
        out_ref[...] = table if opening else table + before_ref[...]


def gram_call(info, before, group, opening):
    count = len(group)
    steps = 3
    if opening:
        block, place = (group[0].shape[0], group[0].shape[1] // steps), lambda i, h: (0, i)
    else:
        block, place = (group[0].shape[0] // steps, group[0].shape[1]), lambda i, h: (i, 0)
    rows = 8 * -(-count // 8)
    pairs = count * (count + 1) // 2
    return pl.pallas_call(
        functools.partial(gram_kernel, count=count, opening=opening),
        grid_spec=pltpu.PrefetchScalarGridSpec(
            num_scalar_prefetch=1,
            grid=(steps,),
            in_specs=[pl.BlockSpec(before.shape, lambda i, h: (0, 0))]
            + [pl.BlockSpec(block, place)] * count,
            out_specs=pl.BlockSpec((rows, 128), lambda i, h: (0, 0)),
            scratch_shapes=[pltpu.VMEM((pairs, 8, 128), f32)],
        ),
        out_shape=jax.ShapeDtypeStruct((rows, 128), f32),
        compiler_params=pltpu.CompilerParams(vmem_limit_bytes=GRAM_LIMIT),
    )(info, before, *group)


def tree_weights(table, member, count):
    row = lax.broadcasted_iota(jnp.int32, table.shape, 0)
    lane = lax.broadcasted_iota(jnp.int32, table.shape, 1)

    def entry(a, b):
        picked = jnp.where((row == a) & (lane == b), table, 0.0)
        return jnp.sum(jnp.sum(picked, axis=1, keepdims=True), axis=0, keepdims=True)

    weights = [1.0 / entry(member ^ j, count) for j in range(count)]
    gram = {}
    for j in range(count):
        for k in range(j, count):
            gram[j, k] = entry(member ^ j, member ^ k) * weights[j] * weights[k]
    left = count
    while left > 1:
        bit = left // 2
        low, high = [], []
        for j in range(bit):
            norm_low = jnp.maximum(gram[j, j], 0.0)
            norm_high = jnp.maximum(gram[j + bit, j + bit], 0.0)
            limit = jnp.sqrt(norm_low) * jnp.sqrt(norm_high)
            product = jnp.clip(gram[j, j + bit], -limit, limit)
            low.append(1.0 - product / (2.0 * (norm_low + eps_adasum)))
            high.append(1.0 - product / (2.0 * (norm_high + eps_adasum)))
        for j in range(count):
            weights[j] = weights[j] * (high if j & bit else low)[j % bit]
        gram = {
            (j, k): low[j] * low[k] * gram[j, k]
            + high[j] * high[k] * gram[j + bit, k + bit]
            + (low[j] * high[k] * gram[j, k + bit] + low[k] * high[j] * gram[k, j + bit])
            for j in range(bit)
            for k in range(j, bit)
        }
        left = bit
    return weights


def update_kernel(info_ref, mine_ref, theirs_ref, *refs, count):
    firsts, seconds = refs[:count], refs[count : 2 * count]
    w1_ref, w2_ref, m1_ref, m2_ref, v1_ref, v2_ref = refs[2 * count : 2 * count + 6]
    outs, weight_ref = refs[2 * count + 6 : -1], refs[-1]

    @pl.when(pl.program_id(0) == 0)
    def _():
        weights = tree_weights(mine_ref[...] + theirs_ref[...], info_ref[0], count)
        for j in range(count):
            weight_ref[j : j + 1, :] = jnp.broadcast_to(weights[j], (1, 128))

    def combine(group):
        return sum(group[j][...] * weight_ref[j : j + 1, 0:1] for j in range(count))

    grad = combine(firsts)
    new = adam_update(grad, w1_ref[0].astype(f32), m1_ref[0], v1_ref[0])
    for n in range(3):
        outs[2 * n][0] = new[n]
    grad = combine(seconds).T
    new = adam_update(grad, w2_ref[0].astype(f32), m2_ref[0], v2_ref[0])
    for n in range(3):
        outs[2 * n + 1][0] = new[n]


def update_call(info, mine, theirs, firsts, seconds, w1, w2, m1, m2, v1, v2):
    count = len(firsts)
    steps = 6
    rows_first, hidden_width = firsts[0].shape
    width, rows_second = seconds[0].shape
    first_block = (rows_first, hidden_width // steps)
    second_block = (width // steps, rows_second)
    first_own = pl.BlockSpec((1,) + first_block, lambda i, h: (0, 0, i))
    second_own = pl.BlockSpec((1, rows_second, width // steps), lambda i, h: (0, 0, i))
    return pl.pallas_call(
        functools.partial(update_kernel, count=count),
        grid_spec=pltpu.PrefetchScalarGridSpec(
            num_scalar_prefetch=1,
            grid=(steps,),
            in_specs=[pl.BlockSpec(mine.shape, lambda i, h: (0, 0))] * 2
            + [pl.BlockSpec(first_block, lambda i, h: (0, i))] * count
            + [pl.BlockSpec(second_block, lambda i, h: (i, 0))] * count
            + [
                pl.BlockSpec((1,) + first_block, lambda i, h: (0, h[1], i)),
                pl.BlockSpec((1, rows_second, width // steps), lambda i, h: (0, h[1], i)),
            ]
            + [first_own, second_own] * 2,
            out_specs=[first_own, second_own] * 3,
            scratch_shapes=[pltpu.VMEM((8 * -(-count // 8), 128), f32)],
        ),
        out_shape=[
            jax.ShapeDtypeStruct((1, rows_first, hidden_width), f32),
            jax.ShapeDtypeStruct((1, rows_second, width), f32),
        ]
        * 3,
        compiler_params=pltpu.CompilerParams(vmem_limit_bytes=UPDATE_LIMIT),
    )(info, mine, theirs, *firsts, *seconds, w1, w2, m1, m2, v1, v2)


def after(value, *others):
    return lax.optimization_barrier((value, *others))[0]


def body(
    tokens,
    assigned,
    gate_prob,
    cotangent,
    weight_in,
    weight_out,
    moment_in,
    moment_out,
    second_in,
    second_out,
):
    experts = lax.axis_size("expert")
    replicas = lax.axis_size("dp")
    top = replicas // 2
    self_index = lax.axis_index("dp")
    expert = lax.axis_index("expert")
    half = self_index // top
    member = self_index % top
    tok_rows, width = tokens.shape
    hidden_width = weight_in.shape[2]
    capacity = 2 * tok_rows // experts
    rows_first = width // replicas
    rows_second = hidden_width // replicas
    w_first = weight_in[0]
    w_second = weight_out[0]
    info = jnp.stack([member, self_index, half]).astype(jnp.int32)

    ids = assigned.reshape(-1, 128)
    far_ids = swap(ids, "dp", top)
    scaled = (after(gate_prob, ids) * cotangent.astype(f32)).astype(bf16)
    far_scaled = swap(scaled, "dp", top)
    table = slot_table(assigned, expert, experts, capacity)
    upstream, own_sent = dispatch(table, scaled, experts)
    inputs = dispatch(table, after(tokens, *own_sent), experts)[0]
    far_tokens = swap(after(tokens, upstream), "dp", top)

    far_table = slot_table(far_ids.reshape(-1, 1), expert, experts, capacity)
    own_in, own_out, partial_out = expert_call(
        "first", info, after(inputs, upstream), upstream, w_first, w_second
    )
    far_scaled = after(far_scaled, partial_out)
    far_upstream = dispatch(far_table, far_scaled, experts)[0]
    far_tokens = after(far_tokens, partial_out)
    far_inputs, far_sent = dispatch(far_table, far_tokens, experts)
    own_in, expert_out = expert_call(
        "second",
        info,
        inputs,
        upstream,
        w_first,
        w_second,
        after(partial_out, *far_sent),
        own_in,
    )

    expert_out = after(expert_out, far_upstream)
    returned = exchange_blocks(
        [expert_out[j * capacity : (j + 1) * capacity] for j in range(experts)]
    )
    far_in, far_out, mine = expert_call(
        "far", info, far_inputs, far_upstream, w_first, w_second, own_in, own_out
    )
    mine = after(mine, returned)

    theirs = swap(mine, "dp", top)
    cross = mine[0] + theirs[0]
    norm_own = mine[1] + theirs[2]
    norm_far = mine[2] + theirs[1]
    coef_own = 1.0 - cross / (2.0 * (norm_own + eps_adasum))
    coef_far = 1.0 - cross / (2.0 * (norm_far + eps_adasum))
    weighted = coef_own * coef_own * norm_own + coef_far * coef_far * norm_far
    norm = jnp.maximum(weighted + 2.0 * coef_own * coef_far * cross, 1e-5 * weighted)
    scale = 16384.0 * lax.rsqrt(jnp.maximum(norm, 1e-12))
    weight_own, weight_far = coef_own * scale, coef_far * scale

    def quarter(own, far, other, axis):
        size = own.shape[axis] // top
        own, far = (
            lax.dynamic_slice_in_dim(x, (member ^ other) * size, size, axis) for x in (own, far)
        )
        return weight_own[0] * own + weight_far[0] * far

    def exchange(own, far, axis):
        received = [quarter(own, far, 0, axis)]
        for other in range(1, top):
            outgoing = quarter(own, far, other, axis).astype(f16)
            received.append(swap(outgoing, "dp", other).astype(f32))
        return received

    firsts = exchange(own_in, far_in, 0)
    seconds = exchange(own_out, far_out, 1)

    products = gram_call(info, scale.reshape(1, 128), firsts, True)
    products = gram_call(info, products, seconds, False)
    bit = 1
    while bit < top:
        products = products + swap(products, "dp", bit)
        bit *= 2
    new = update_call(
        info,
        products,
        swap(products, "dp", top),
        firsts,
        seconds,
        weight_in,
        weight_out,
        moment_in,
        moment_out,
        second_in,
        second_out,
    )

    picked = contract_rows(table, jnp.concatenate(returned, axis=0))
    combined = (gate_prob * picked).astype(bf16)
    return (combined, *new)


def solution(mesh):
    row_spec = P(("dp", "expert"), None)
    owner_spec = P("expert", "dp", None)
    return jax.shard_map(
        body,
        mesh=mesh,
        in_specs=(row_spec,) * 4 + (P("expert", None, None),) * 2 + (owner_spec,) * 4,
        out_specs=(row_spec,) + (owner_spec,) * 6,
        check_vma=False,
    )
```

time: 236 us -> 216 us (0.915)
  waiting for transfers between devices: 108 us -> 73.6 us
  starting transfers between devices: 19.8 us -> 35.5 us
  between operations: 5.13 us -> 1.28 us
  local copies, waits for them, and re-layouts: 4.27 us -> 6.79 us
    ppermute x28, waiting for transfers between devices: 108 us -> 73.6 us  [swap(): lax.ppermute(x, axis, [(i, i ^ offset) for i in range(lax.axis_size(axis))])]
    ppermute x28, starting transfers between devices: 19.8 us -> 35.5 us  [swap(): lax.ppermute(x, axis, [(i, i ^ offset) for i in range(lax.axis_size(axis))])]
    pallas_call x3 -> x5, Pallas kernels: 59 us -> 63.5 us  [the longest x3 58.9 us: expert_call(): pl.pallas_call(functools.partial(expert_kernel, steps=steps, kind=kind),...]
    pallas_call x1, Pallas kernels: 9.07 us -> 6.12 us  [update_call(): pl.pallas_call(functools.partial(update_kernel, count=count), grid_spec=p...]
    unnamed x12 -> x44, local copies, waits for them, and re-layouts: 0.45 us -> 2.83 us
  transfers between devices with their start and end apart: 28 -> 28, of which waited for: 13 -> 12; matrix products, arithmetic and copies ran while one was open for 12% -> 13% of each run, Pallas kernels for 14% -> 28%
where the time goes in v1:
time: 216 us
  waiting for transfers between devices  73.6 us (34%)
  Pallas kernels  69.6 us (32%)
  starting transfers between devices  35.5 us (16%)
  other arithmetic  20.6 us (10%)
  matrix products  8.5 us (4%)
  local copies, waits for them, and re-layouts  6.79 us (3%)
    ppermute x28, waiting for transfers between devices, swap(): lax.ppermute(x, axis, [(i, i ^ offset) for i in range(lax.axis_size(axis))])  73.6 us
    pallas_call x3, Pallas kernels, expert_call(): pl.pallas_call(functools.partial(expert_kernel, steps=steps, kind=kind),...  58.9 us
    ppermute x28, starting transfers between devices, swap(): lax.ppermute(x, axis, [(i, i ^ offset) for i in range(lax.axis_size(axis))])  35.5 us
    convert_element_type x2, other arithmetic, exchange(): outgoing = quarter(own, far, other, axis).astype(f16)  9.87 us
    dot_general x4, matrix products, place_rows(): sent = jnp.dot(table, rows, preferred_element_type=f32).astype(bf16)  6.38 us
    pallas_call x1, Pallas kernels, update_call(): pl.pallas_call(functools.partial(update_kernel, count=count), grid_spec=p...  6.12 us
    another operation x4, other arithmetic  5.09 us
    pallas_call x2, Pallas kernels, gram_call(): pl.pallas_call(functools.partial(gram_kernel, count=count, opening=openin...  4.61 us
  transfers between devices with their start and end apart: 28, of which 12 were waited for; matrix products, arithmetic and copies ran while one was open for 13% of the time, Pallas kernels for 28%

profile of v1, /device:TPU:0, one launch (start us, length us, event | category | flops | bytes accessed | tf_op | source)
XLA Modules:
  0.0 215.8 jit_solution(1603809258805450480)
XLA Ops:
  0.6 4.1 %collective-permute-start.6 = (s32[4,128]{1,0:T(4,128)}, s32[4,128]{1,0:T(4,128)S(1)}, u32[]{:S(2)}, u32[]{:S(2)}) collective-permute-start(s32[4,128]{1,0:T(4,128)} %bitcast.116), channel_id=1, source_target_pairs={{0,16},{4,20},{8,24},{12,28},{16,0},{20,4},{24,8},{28,12},{1,17},{... | collective-permute-start | bytes 6152 | tf_op jit(solution)/shard_map/ppermute | solution.py:25
  11.8 2.2 fusion.6
  17.0 2.3 %reduce-window.16 = s32[4,4,128]{2,1,0:T(4,128)S(1)} reduce-window(s32[4,4,128]{2,1,0:T(4,128)} %fusion.30, s32[]{:T(128)} %constant.48.clone.1), window={size=1x1x128 pad=0_0x0_0x127_0}, to_apply=%region_3.4 | reduce-window | flops 260096 | bytes 16388 | tf_op jit(solution)/shard_map/reduce-window.2
  23.2 7.0 %collective-permute-done.4 = bf16[256,768]{1,0:T(8,128)(2,1)S(1)} collective-permute-done((bf16[256,768]{1,0:T(8,128)(2,1)S(1)}, bf16[256,768]{1,0:T(8,128)(2,1)S(1)}, u32[]{:S(2)}, u32[]{:S(2)}) %collective-permute-start.4) | collective-permute-done | bytes 393248 | tf_op jit(solution)/shard_map/ppermute | solution.py:25
  31.4 2.6 %collective-permute-start.7 = (bf16[512,768]{1,0:T(8,128)(2,1)S(1)}, bf16[512,768]{1,0:T(8,128)(2,1)S(1)}, u32[]{:S(2)}, u32[]{:S(2)}) collective-permute-start(bf16[512,768]{1,0:T(8,128)(2,1)S(1)} %copy-done.11), channel_id=1, source_target_pairs={{0,16},{4,20},{8,24},{12,28},{16,0},{20,4},{24,8},{28,12},{1,17},{... | collective-permute-start | bytes 2359304 | tf_op jit(solution)/shard_map/ppermute | solution.py:25
  34.0 4.1 %collective-permute-done.2 = bf16[256,768]{1,0:T(8,128)(2,1)} collective-permute-done((bf16[256,768]{1,0:T(8,128)(2,1)}, bf16[256,768]{1,0:T(8,128)(2,1)}, u32[]{:S(2)}, u32[]{:S(2)}) %collective-permute-start.2) | collective-permute-done | bytes 393248 | tf_op jit(solution)/shard_map/ppermute | solution.py:25
  38.1 8.7 %collective-permute-done.1 = bf16[256,768]{1,0:T(8,128)(2,1)S(1)} collective-permute-done((bf16[256,768]{1,0:T(8,128)(2,1)}, bf16[256,768]{1,0:T(8,128)(2,1)S(1)}, u32[]{:S(2)}, u32[]{:S(2)}) %collective-permute-start.1) | collective-permute-done | bytes 393248 | tf_op jit(solution)/shard_map/ppermute | solution.py:25
  47.8 18.2 %shard_map.153 = (f32[384,3072]{1,0:T(8,128)}, f32[768,1536]{1,0:T(8,128)}, f32[1024,768]{1,0:T(8,128)}) custom-call(s32[3]{0:T(128)S(1)} %pad_add_fusion.info_ref, bf16[1024,768]{1,0:T(8,128)(2,1)S(1)} %pad_maximum_fusion.x_ref, bf16[1024,768]{1,0:T(8,128)(2,1)S(1)} %pad_maximum_fusion.1.u_ref, bf16[768,3072]{1,0:T(8,128)(2,1)} %bitcast.106, ...), custom_call_target="tpu_custom_call" | custom-call | flops 1024 | bytes 1024 | tf_op jit(solution)/shard_map/pallas_call | solution.py:213
  66.1 2.2 fusion.8
  70.3 6.3 %collective-permute-done.7 = bf16[512,768]{1,0:T(8,128)(2,1)S(1)} collective-permute-done((bf16[512,768]{1,0:T(8,128)(2,1)S(1)}, bf16[512,768]{1,0:T(8,128)(2,1)S(1)}, u32[]{:S(2)}, u32[]{:S(2)}) %collective-permute-start.7) | collective-permute-done | bytes 786464 | tf_op jit(solution)/shard_map/ppermute | solution.py:25
  79.4 15.3 %shard_map.154 = (f32[384,3072]{1,0:T(8,128)}, bf16[1024,768]{1,0:T(8,128)(2,1)S(1)}) custom-call(s32[3]{0:T(128)S(1)} %pad_add_fusion.info_ref, bf16[1024,768]{1,0:T(8,128)(2,1)S(1)} %pad_maximum_fusion.x_ref, bf16[1024,768]{1,0:T(8,128)(2,1)S(1)} %pad_maximum_fusion.1.u_ref, bf16[768,3072]{1,0:T(8,128)(2,1)} %bitcast.107, ...), custom_call_target="tpu_custom_call", output_to_operand_aliasing={{0}: (6, {})} | custom-call | flops 1024 | bytes 1024 | tf_op jit(solution)/shard_map/pallas_call | solution.py:213
  97.8 7.4 %collective-permute-done.16 = bf16[256,768]{1,0:T(8,128)(2,1)S(1)} collective-permute-done((bf16[256,768]{1,0:T(8,128)(2,1)S(1)}, bf16[256,768]{1,0:T(8,128)(2,1)S(1)}, u32[]{:S(2)}, u32[]{:S(2)}) %collective-permute-start.16) | collective-permute-done | bytes 393248 | tf_op jit(solution)/shard_map/ppermute | solution.py:25
  105.3 25.3 %shard_map.155 = (f32[384,3072]{1,0:T(8,128)}, f32[768,1536]{1,0:T(8,128)}, f32[8,128]{1,0:T(8,128)S(1)}) custom-call(s32[3]{0:T(128)S(1)} %pad_add_fusion.info_ref, bf16[1024,768]{1,0:T(8,128)(2,1)S(1)} %pad_maximum_fusion.3.x_ref, bf16[1024,768]{1,0:T(8,128)(2,1)S(1)} %pad_maximum_fusion.2.u_ref, bf16[768,3072]{1,0:T(8,128)(2,1)} %bitcast.108, ...), custom_call_target="tpu_custom_call" | custom-call | flops 1024 | bytes 1024 | tf_op jit(solution)/shard_map/pallas_call | solution.py:213
  131.7 3.1 %collective-permute-start.18 = (f32[8,128]{1,0:T(8,128)S(1)}, f32[8,128]{1,0:T(8,128)S(1)}, u32[]{:S(2)}, u32[]{:S(2)}) collective-permute-start(f32[8,128]{1,0:T(8,128)S(1)} %get-tuple-element.44), channel_id=1, source_target_pairs={{0,16},{4,20},{8,24},{12,28},{16,0},{20,4},{24,8},{28,12},{1,17},{... | collective-permute-start | bytes 12296 | tf_op jit(solution)/shard_map/ppermute | solution.py:25
  136.9 4.8 %add_convert_fusion.3 = (f16[96,3072]{1,0:T(8,128)(2,1)S(1)}, f16[96,3072]{1,0:T(8,128)(2,1)S(1)}, f16[96,3072]{1,0:T(8,128)(2,1)S(1)}, f32[96,3072]{1,0:T(8,128)S(1)}) fusion(f32[384,3072]{1,0:T(8,128)} %get-tuple-element.45, s32[]{:T(128)S(6)} %select_n.48, f32[384,3072]{1,0:T(8,128)} %get-tuple-element.41.rest_0_, f32[]{:T(128)S(1)} %bitcast.127, ...), kind=kLoop, calls=%fused_computation.28 | loop fusion | flops 4423680 | bytes 12386328 | tf_op jit(solution)/shard_map/convert_element_type | solution.py:469
  141.8 1.9 collective-permute-start.19
  145.3 5.1 %add_convert_fusion = (f16[768,384]{1,0:T(8,128)(2,1)S(1)}, f16[768,384]{1,0:T(8,128)(2,1)S(1)}, f16[768,384]{1,0:T(8,128)(2,1)S(1)}, f32[768,384]{1,0:T(8,128)S(1)}) fusion(f32[768,1536]{1,0:T(8,128)} %get-tuple-element.46, s32[]{:T(128)S(6)} %select_n.52, f32[768,1536]{1,0:T(8,128)} %get-tuple-element.42.rest_1_, f32[]{:T(128)} %bitcast.128, ...), kind=kLoop, calls=%fused_computation.24 | loop fusion | flops 4423680 | bytes 12386328 | tf_op jit(solution)/shard_map/convert_element_type | solution.py:469
  150.4 1.9 collective-permute-start.22
  153.8 15.4 %collective-permute-done.19 = f16[96,3072]{1,0:T(8,128)(2,1)S(1)} collective-permute-done((f16[96,3072]{1,0:T(8,128)(2,1)S(1)}, f16[96,3072]{1,0:T(8,128)(2,1)S(1)}, u32[]{:S(2)}, u32[]{:S(2)}) %collective-permute-start.19) | collective-permute-done | bytes 589856 | tf_op jit(solution)/shard_map/ppermute | solution.py:25
  169.2 2.8 %collective-permute-start.24 = (f16[768,384]{1,0:T(8,128)(2,1)S(1)}, f16[768,384]{1,0:T(8,128)(2,1)S(1)}, u32[]{:S(2)}, u32[]{:S(2)}) collective-permute-start(f16[768,384]{1,0:T(8,128)(2,1)S(1)} %get-tuple-element.58), channel_id=1, source_target_pairs={{0,12},{4,8},{8,4},{12,0},{16,28},{20,24},{24,20},{28,16},{1,13},{... | collective-permute-start | bytes 1769480 | tf_op jit(solution)/shard_map/ppermute | solution.py:25
  173.1 2.6 %shard_map.156.before_ref = f32[8,128]{1,0:T(8,128)S(1)} custom-call(s32[3]{0:T(128)S(1)} %pad_add_fusion.info_ref, f32[1,128]{1,0:T(1,128)S(1)} %rsqrt_multiply_fusion.1.before_ref, f32[96,3072]{1,0:T(8,128)S(1)} %get-tuple-element.65.refs_0_, f32[96,3072]{1,0:T(8,128)S(1)} %convert_element_type.85.refs_1_, f32[96,3072]{1,0:T(8,128)S(1)} %convert_element_type.87.refs_2_, ...), custom_call_target="tpu_custom_call" | custom-call | tf_op jit(solution)/shard_map/pallas_call | solution.py:269
  175.8 6.7 %collective-permute-done.22 = f16[768,384]{1,0:T(8,128)(2,1)S(1)} collective-permute-done((f16[768,384]{1,0:T(8,128)(2,1)S(1)}, f16[768,384]{1,0:T(8,128)(2,1)S(1)}, u32[]{:S(2)}, u32[]{:S(2)}) %collective-permute-start.22) | collective-permute-done | bytes 589856 | tf_op jit(solution)/shard_map/ppermute | solution.py:25
  182.5 2.7 %collective-permute-done.23 = f16[768,384]{1,0:T(8,128)(2,1)S(1)} collective-permute-done((f16[768,384]{1,0:T(8,128)(2,1)S(1)}, f16[768,384]{1,0:T(8,128)(2,1)S(1)}, u32[]{:S(2)}, u32[]{:S(2)}) %collective-permute-start.23) | collective-permute-done | bytes 589856 | tf_op jit(solution)/shard_map/ppermute | solution.py:25
  185.3 9.6 %collective-permute-done.24 = f16[768,384]{1,0:T(8,128)(2,1)S(1)} collective-permute-done((f16[768,384]{1,0:T(8,128)(2,1)S(1)}, f16[768,384]{1,0:T(8,128)(2,1)S(1)}, u32[]{:S(2)}, u32[]{:S(2)}) %collective-permute-start.24) | collective-permute-done | bytes 589856 | tf_op jit(solution)/shard_map/ppermute | solution.py:25
  195.1 2.0 shard_map.157
  197.1 1.6 collective-permute-start.25
  198.7 2.1 collective-permute-done.25
  200.8 1.6 collective-permute-start.26
  202.4 2.0 collective-permute-done.26
  204.4 2.6 %collective-permute-start.27 = (f32[8,128]{1,0:T(8,128)S(1)}, f32[8,128]{1,0:T(8,128)S(1)}, u32[]{:S(2)}, u32[]{:S(2)}) collective-permute-start(f32[8,128]{1,0:T(8,128)S(1)} %add.160.mine_ref), channel_id=1, source_target_pairs={{0,16},{4,20},{8,24},{12,28},{16,0},{20,4},{24,8},{28,12},{1,17},{... | collective-permute-start | bytes 12296 | tf_op jit(solution)/shard_map/ppermute | solution.py:25
  207.1 2.1 multiply_convert_fusion
  209.5 6.1 %shard_map.158 = (f32[1,96,3072]{2,1,0:T(8,128)}, f32[1,384,768]{2,1,0:T(8,128)}, f32[1,96,3072]{2,1,0:T(8,128)}, f32[1,384,768]{2,1,0:T(8,128)}, f32[1,96,3072]{2,1,0:T(8,128)}, /*index=5*/f32[1,384,768]{2,1,0:T(8,128)}) custom-call(s32[3]{0:T(128)S(1)} %pad_add_fusion.info_ref, f32[8,128]{1,0:T(8,128)S(1)} %add.160.mine_ref, ...), custom_call_target="tpu_custom_call" | custom-call | tf_op jit(solution)/shard_map/pallas_call | solution.py:354
  (120 shorter events, 32.2 us)
Async XLA Ops:
  0.6 14.4 %collective-permute-start.6 = (s32[4,128]{1,0:T(4,128)}, s32[4,128]{1,0:T(4,128)S(1)}, u32[]{:S(2)}, u32[]{:S(2)}) collective-permute-start(s32[4,128]{1,0:T(4,128)} %bitcast.116), channel_id=1, source_target_pairs={{0,16},{4,20},{8,24},{12,28},{16,0},{20,4},{24,8},{28,12},{1,17},{... | collective-permute-start | bytes 6152 | tf_op jit(solution)/shard_map/ppermute | solution.py:25
  6.1 60.0 %collective-permute-start.8 = (bf16[512,768]{1,0:T(8,128)(2,1)S(1)}, bf16[512,768]{1,0:T(8,128)(2,1)}, u32[]{:S(2)}, u32[]{:S(2)}) collective-permute-start(bf16[512,768]{1,0:T(8,128)(2,1)S(1)} %multiply_convert_fusion.1), channel_id=1, source_target_pairs={{0,16},{4,20},{8,24},{12,28},{16,0},{20,4},{24,8},{28,12},{1,17},{... | collective-permute-start | bytes 2359304 | tf_op jit(solution)/shard_map/ppermute | solution.py:25
  9.8 12.4 %collective-permute-start.5 = (bf16[256,768]{1,0:T(8,128)(2,1)}, bf16[256,768]{1,0:T(8,128)(2,1)S(1)}, u32[]{:S(2)}, u32[]{:S(2)}) collective-permute-start(bf16[256,768]{1,0:T(8,128)(2,1)} %get-tuple-element.82), channel_id=1, source_target_pairs={{0,3},{1,2},{2,1},{3,0},{4,7},{5,6},{6,5},{7,4},{8,11},{9,10},{10,... | collective-permute-start | bytes 1179656 | tf_op jit(solution)/shard_map/ppermute | solution.py:25
  10.5 19.7 %collective-permute-start.4 = (bf16[256,768]{1,0:T(8,128)(2,1)S(1)}, bf16[256,768]{1,0:T(8,128)(2,1)S(1)}, u32[]{:S(2)}, u32[]{:S(2)}) collective-permute-start(bf16[256,768]{1,0:T(8,128)(2,1)S(1)} %get-tuple-element.83), channel_id=1, source_target_pairs={{0,2},{1,3},{2,0},{3,1},{4,6},{5,7},{6,4},{7,5},{8,10},{9,11},{10,... | collective-permute-start | bytes 1179656 | tf_op jit(solution)/shard_map/ppermute | solution.py:25
  11.7 18.6 %collective-permute-start.3 = (bf16[256,768]{1,0:T(8,128)(2,1)S(1)}, bf16[256,768]{1,0:T(8,128)(2,1)S(1)}, u32[]{:S(2)}, u32[]{:S(2)}) collective-permute-start(bf16[256,768]{1,0:T(8,128)(2,1)S(1)} %get-tuple-element.84), channel_id=1, source_target_pairs={{0,1},{1,0},{2,3},{3,2},{4,5},{5,4},{6,7},{7,6},{8,9},{9,8},{10,11... | collective-permute-start | bytes 1179656 | tf_op jit(solution)/shard_map/ppermute | solution.py:25
  15.0 23.0 %collective-permute-start.2 = (bf16[256,768]{1,0:T(8,128)(2,1)}, bf16[256,768]{1,0:T(8,128)(2,1)}, u32[]{:S(2)}, u32[]{:S(2)}) collective-permute-start(bf16[256,768]{1,0:T(8,128)(2,1)} %get-tuple-element.79), channel_id=1, source_target_pairs={{0,3},{1,2},{2,1},{3,0},{4,7},{5,6},{6,5},{7,4},{8,11},{9,10},{10,... | collective-permute-start | bytes 1179656 | tf_op jit(solution)/shard_map/ppermute | solution.py:25
  22.2 24.5 %collective-permute-start.1 = (bf16[256,768]{1,0:T(8,128)(2,1)}, bf16[256,768]{1,0:T(8,128)(2,1)S(1)}, u32[]{:S(2)}, u32[]{:S(2)}) collective-permute-start(bf16[256,768]{1,0:T(8,128)(2,1)} %get-tuple-element.80), channel_id=1, source_target_pairs={{0,2},{1,3},{2,0},{3,1},{4,6},{5,7},{6,4},{7,5},{8,10},{9,11},{10,... | collective-permute-start | bytes 1179656 | tf_op jit(solution)/shard_map/ppermute | solution.py:25
  30.2 16.5 %collective-permute-start = (bf16[256,768]{1,0:T(8,128)(2,1)}, bf16[256,768]{1,0:T(8,128)(2,1)S(1)}, u32[]{:S(2)}, u32[]{:S(2)}) collective-permute-start(bf16[256,768]{1,0:T(8,128)(2,1)} %get-tuple-element.81), channel_id=1, source_target_pairs={{0,1},{1,0},{2,3},{3,2},{4,5},{5,4},{6,7},{7,6},{8,9},{9,8},{10,11... | collective-permute-start | bytes 1179656 | tf_op jit(solution)/shard_map/ppermute | solution.py:25
  31.4 45.2 %collective-permute-start.7 = (bf16[512,768]{1,0:T(8,128)(2,1)S(1)}, bf16[512,768]{1,0:T(8,128)(2,1)S(1)}, u32[]{:S(2)}, u32[]{:S(2)}) collective-permute-start(bf16[512,768]{1,0:T(8,128)(2,1)S(1)} %copy-done.11), channel_id=1, source_target_pairs={{0,16},{4,20},{8,24},{12,28},{16,0},{20,4},{24,8},{28,12},{1,17},{... | collective-permute-start | bytes 2359304 | tf_op jit(solution)/shard_map/ppermute | solution.py:25
  68.4 26.3 %collective-permute-start.11 = (bf16[256,768]{1,0:T(8,128)(2,1)S(1)}, bf16[256,768]{1,0:T(8,128)(2,1)S(1)}, u32[]{:S(2)}, u32[]{:S(2)}) collective-permute-start(bf16[256,768]{1,0:T(8,128)(2,1)S(1)} %get-tuple-element.71), channel_id=1, source_target_pairs={{0,3},{1,2},{2,1},{3,0},{4,7},{5,6},{6,5},{7,4},{8,11},{9,10},{10,... | collective-permute-start | bytes 1179656 | tf_op jit(solution)/shard_map/ppermute | solution.py:25
  69.5 25.5 %collective-permute-start.10 = (bf16[256,768]{1,0:T(8,128)(2,1)S(1)}, bf16[256,768]{1,0:T(8,128)(2,1)S(1)}, u32[]{:S(2)}, u32[]{:S(2)}) collective-permute-start(bf16[256,768]{1,0:T(8,128)(2,1)S(1)} %get-tuple-element.72), channel_id=1, source_target_pairs={{0,2},{1,3},{2,0},{3,1},{4,6},{5,7},{6,4},{7,5},{8,10},{9,11},{10,... | collective-permute-start | bytes 1179656 | tf_op jit(solution)/shard_map/ppermute | solution.py:25
  70.0 25.0 %collective-permute-start.9 = (bf16[256,768]{1,0:T(8,128)(2,1)S(1)}, bf16[256,768]{1,0:T(8,128)(2,1)S(1)}, u32[]{:S(2)}, u32[]{:S(2)}) collective-permute-start(bf16[256,768]{1,0:T(8,128)(2,1)S(1)} %get-tuple-element.73), channel_id=1, source_target_pairs={{0,1},{1,0},{2,3},{3,2},{4,5},{5,4},{6,7},{7,6},{8,9},{9,8},{10,11... | collective-permute-start | bytes 1179656 | tf_op jit(solution)/shard_map/ppermute | solution.py:25
  77.8 20.0 %collective-permute-start.17 = (bf16[256,768]{1,0:T(8,128)(2,1)S(1)}, bf16[256,768]{1,0:T(8,128)(2,1)S(1)}, u32[]{:S(2)}, u32[]{:S(2)}) collective-permute-start(bf16[256,768]{1,0:T(8,128)(2,1)S(1)} %get-tuple-element.74), channel_id=1, source_target_pairs={{0,3},{1,2},{2,1},{3,0},{4,7},{5,6},{6,5},{7,4},{8,11},{9,10},{10,... | collective-permute-start | bytes 1179656 | tf_op jit(solution)/shard_map/ppermute | solution.py:25
  77.9 27.3 %collective-permute-start.16 = (bf16[256,768]{1,0:T(8,128)(2,1)S(1)}, bf16[256,768]{1,0:T(8,128)(2,1)S(1)}, u32[]{:S(2)}, u32[]{:S(2)}) collective-permute-start(bf16[256,768]{1,0:T(8,128)(2,1)S(1)} %get-tuple-element.75), channel_id=1, source_target_pairs={{0,2},{1,3},{2,0},{3,1},{4,6},{5,7},{6,4},{7,5},{8,10},{9,11},{10,... | collective-permute-start | bytes 1179656 | tf_op jit(solution)/shard_map/ppermute | solution.py:25
  94.7 10.5 %collective-permute-start.15 = (bf16[256,768]{1,0:T(8,128)(2,1)S(1)}, bf16[256,768]{1,0:T(8,128)(2,1)S(1)}, u32[]{:S(2)}, u32[]{:S(2)}) collective-permute-start(bf16[256,768]{1,0:T(8,128)(2,1)S(1)} %get-tuple-element.76), channel_id=1, source_target_pairs={{0,1},{1,0},{2,3},{3,2},{4,5},{5,4},{6,7},{7,6},{8,9},{9,8},{10,11... | collective-permute-start | bytes 1179656 | tf_op jit(solution)/shard_map/ppermute | solution.py:25
  95.9 34.7 %collective-permute-start.14 = (bf16[256,768]{1,0:T(8,128)(2,1)S(1)}, bf16[256,768]{1,0:T(8,128)(2,1)S(1)}, u32[]{:S(2)}, u32[]{:S(2)}) collective-permute-start(bf16[256,768]{1,0:T(8,128)(2,1)S(1)} %get-tuple-element.67), channel_id=1, source_target_pairs={{0,3},{1,2},{2,1},{3,0},{4,7},{5,6},{6,5},{7,4},{8,11},{9,10},{10,... | collective-permute-start | bytes 1179656 | tf_op jit(solution)/shard_map/ppermute | solution.py:25
  97.1 33.6 %collective-permute-start.13 = (bf16[256,768]{1,0:T(8,128)(2,1)S(1)}, bf16[256,768]{1,0:T(8,128)(2,1)S(1)}, u32[]{:S(2)}, u32[]{:S(2)}) collective-permute-start(bf16[256,768]{1,0:T(8,128)(2,1)S(1)} %get-tuple-element.68), channel_id=1, source_target_pairs={{0,2},{1,3},{2,0},{3,1},{4,6},{5,7},{6,4},{7,5},{8,10},{9,11},{10,... | collective-permute-start | bytes 1179656 | tf_op jit(solution)/shard_map/ppermute | solution.py:25
  97.8 32.9 %collective-permute-start.12 = (bf16[256,768]{1,0:T(8,128)(2,1)S(1)}, bf16[256,768]{1,0:T(8,128)(2,1)S(1)}, u32[]{:S(2)}, u32[]{:S(2)}) collective-permute-start(bf16[256,768]{1,0:T(8,128)(2,1)S(1)} %get-tuple-element.69), channel_id=1, source_target_pairs={{0,1},{1,0},{2,3},{3,2},{4,5},{5,4},{6,7},{7,6},{8,9},{9,8},{10,11... | collective-permute-start | bytes 1179656 | tf_op jit(solution)/shard_map/ppermute | solution.py:25
  131.7 4.7 %collective-permute-start.18 = (f32[8,128]{1,0:T(8,128)S(1)}, f32[8,128]{1,0:T(8,128)S(1)}, u32[]{:S(2)}, u32[]{:S(2)}) collective-permute-start(f32[8,128]{1,0:T(8,128)S(1)} %get-tuple-element.44), channel_id=1, source_target_pairs={{0,16},{4,20},{8,24},{12,28},{16,0},{20,4},{24,8},{28,12},{1,17},{... | collective-permute-start | bytes 12296 | tf_op jit(solution)/shard_map/ppermute | solution.py:25
  141.8 27.5 %collective-permute-start.19 = (f16[96,3072]{1,0:T(8,128)(2,1)S(1)}, f16[96,3072]{1,0:T(8,128)(2,1)S(1)}, u32[]{:S(2)}, u32[]{:S(2)}) collective-permute-start(f16[96,3072]{1,0:T(8,128)(2,1)S(1)} %get-tuple-element.64), channel_id=1, source_target_pairs={{0,4},{4,0},{8,12},{12,8},{16,20},{20,16},{24,28},{28,24},{1,5},{5... | collective-permute-start | bytes 1769480 | tf_op jit(solution)/shard_map/ppermute | solution.py:25
  143.6 29.3 %collective-permute-start.20 = (f16[96,3072]{1,0:T(8,128)(2,1)S(1)}, f16[96,3072]{1,0:T(8,128)(2,1)S(1)}, u32[]{:S(2)}, u32[]{:S(2)}) collective-permute-start(f16[96,3072]{1,0:T(8,128)(2,1)S(1)} %get-tuple-element.63), channel_id=1, source_target_pairs={{0,8},{4,12},{8,0},{12,4},{16,24},{20,28},{24,16},{28,20},{1,9},{5... | collective-permute-start | bytes 1769480 | tf_op jit(solution)/shard_map/ppermute | solution.py:25
  145.2 27.8 %collective-permute-start.21 = (f16[96,3072]{1,0:T(8,128)(2,1)S(1)}, f16[96,3072]{1,0:T(8,128)(2,1)S(1)}, u32[]{:S(2)}, u32[]{:S(2)}) collective-permute-start(f16[96,3072]{1,0:T(8,128)(2,1)S(1)} %get-tuple-element.62), channel_id=1, source_target_pairs={{0,12},{4,8},{8,4},{12,0},{16,28},{20,24},{24,20},{28,16},{1,13},{... | collective-permute-start | bytes 1769480 | tf_op jit(solution)/shard_map/ppermute | solution.py:25
  150.4 32.0 %collective-permute-start.22 = (f16[768,384]{1,0:T(8,128)(2,1)S(1)}, f16[768,384]{1,0:T(8,128)(2,1)S(1)}, u32[]{:S(2)}, u32[]{:S(2)}) collective-permute-start(f16[768,384]{1,0:T(8,128)(2,1)S(1)} %get-tuple-element.60), channel_id=1, source_target_pairs={{0,4},{4,0},{8,12},{12,8},{16,20},{20,16},{24,28},{28,24},{1,5},{5... | collective-permute-start | bytes 1769480 | tf_op jit(solution)/shard_map/ppermute | solution.py:25
  152.3 33.0 %collective-permute-start.23 = (f16[768,384]{1,0:T(8,128)(2,1)S(1)}, f16[768,384]{1,0:T(8,128)(2,1)S(1)}, u32[]{:S(2)}, u32[]{:S(2)}) collective-permute-start(f16[768,384]{1,0:T(8,128)(2,1)S(1)} %get-tuple-element.59), channel_id=1, source_target_pairs={{0,8},{4,12},{8,0},{12,4},{16,24},{20,28},{24,16},{28,20},{1,9},{5... | collective-permute-start | bytes 1769480 | tf_op jit(solution)/shard_map/ppermute | solution.py:25
  169.2 25.7 %collective-permute-start.24 = (f16[768,384]{1,0:T(8,128)(2,1)S(1)}, f16[768,384]{1,0:T(8,128)(2,1)S(1)}, u32[]{:S(2)}, u32[]{:S(2)}) collective-permute-start(f16[768,384]{1,0:T(8,128)(2,1)S(1)} %get-tuple-element.58), channel_id=1, source_target_pairs={{0,12},{4,8},{8,4},{12,0},{16,28},{20,24},{24,20},{28,16},{1,13},{... | collective-permute-start | bytes 1769480 | tf_op jit(solution)/shard_map/ppermute | solution.py:25
  185.2 21.8 %copy-start.17 = (bf16[256,768]{1,0:T(8,128)(2,1)S(1)}, bf16[256,768]{1,0:T(8,128)(2,1)}, u32[]{:S(2)}) copy-start(bf16[256,768]{1,0:T(8,128)(2,1)} %copy-done.16) | copy-start | bytes 1179652
  195.0 14.3 %copy-start.3 = (f32[1,384,768]{2,1,0:T(8,128)S(1)}, f32[1,384,768]{2,1,0:T(8,128)}, u32[]{:S(2)}) copy-start(f32[1,384,768]{2,1,0:T(8,128)} %refs_13_.1) | copy-start | bytes 3538948
  195.1 14.2 %slice-start = ((s8[4718592]{0:T(1024)(128)(4,1)}), s8[4194304]{0:T(1024)(128)(4,1)S(1)}, s32[]{:S(2)}) async-start(s8[4718592]{0:T(1024)(128)(4,1)} %bitcast.109), calls=%async_computation | async-start | bytes 8388608
  195.1 14.2 %slice-start.2 = ((s8[4718592]{0:T(1024)(128)(4,1)}), s8[4194304]{0:T(1024)(128)(4,1)S(1)}, s32[]{:S(2)}) async-start(s8[4718592]{0:T(1024)(128)(4,1)} %bitcast.114), calls=%async_computation.2 | async-start | bytes 8388608
  197.1 3.7 %collective-permute-start.25 = (f32[8,128]{1,0:T(8,128)S(1)}, f32[8,128]{1,0:T(8,128)S(1)}, u32[]{:S(2)}, u32[]{:S(2)}) collective-permute-start(f32[8,128]{1,0:T(8,128)S(1)} %shard_map.157), channel_id=1, source_target_pairs={{0,4},{4,0},{8,12},{12,8},{16,20},{20,16},{24,28},{28,24},{1,5},{5... | collective-permute-start | bytes 12296 | tf_op jit(solution)/shard_map/ppermute | solution.py:25
  200.8 3.6 %collective-permute-start.26 = (f32[8,128]{1,0:T(8,128)S(1)}, f32[8,128]{1,0:T(8,128)S(1)}, u32[]{:S(2)}, u32[]{:S(2)}) collective-permute-start(f32[8,128]{1,0:T(8,128)S(1)} %add.159), channel_id=1, source_target_pairs={{0,8},{4,12},{8,0},{12,4},{16,24},{20,28},{24,16},{28,20},{1,9},{5... | collective-permute-start | bytes 12296 | tf_op jit(solution)/shard_map/ppermute | solution.py:25
  204.4 4.9 %collective-permute-start.27 = (f32[8,128]{1,0:T(8,128)S(1)}, f32[8,128]{1,0:T(8,128)S(1)}, u32[]{:S(2)}, u32[]{:S(2)}) collective-permute-start(f32[8,128]{1,0:T(8,128)S(1)} %add.160.mine_ref), channel_id=1, source_target_pairs={{0,16},{4,20},{8,24},{12,28},{16,0},{20,4},{24,8},{28,12},{1,17},{... | collective-permute-start | bytes 12296 | tf_op jit(solution)/shard_map/ppermute | solution.py:25
  (18 other events, 90.7 us)

commit v2 on v1

--- a/solution.py
+++ b/solution.py
@@ -86,7 +86,9 @@
 def expert_kernel(info_ref, x_ref, u_ref, w1_ref, w2_ref, *rest, steps, kind):
     if kind == "first":
         gi_ref, go_ref, sum_ref, xt_ref, ut_ref = rest
-    elif kind == "second":
+    elif kind == "middle":
+        before_ref, _, _, gi_ref, go_ref, sum_ref, xt_ref = rest
+    elif kind == "last":
         before_ref, _, gi_ref, out_ref, xt_ref, sum_ref = rest
     else:
         own_gi_ref, own_go_ref, gi_ref, go_ref, stat_ref, xt_ref, ut_ref, acc_ref = rest
@@ -97,7 +99,7 @@
     def _():
         start = pl.multiple_of(info_ref[2] * half_width, half_width)
         xt_ref[...] = x_ref[:, pl.ds(start, half_width)].T
-        if kind != "second":
+        if kind in ("first", "far"):
             ut_ref[...] = u_ref[...].T
 
     pre = jnp.dot(x_ref[...], w1_ref[...], preferred_element_type=f32)
@@ -111,6 +113,9 @@
 
     if kind == "first":
         go_ref[...] = jnp.dot(ut_ref[...], hidden, preferred_element_type=f32)
+    elif kind == "middle":
+        go_ref[...] = jnp.dot(u_ref[...].T, hidden, preferred_element_type=f32)
+
     elif kind == "far":
 
         @pl.when(step < steps // 2)
@@ -153,7 +158,7 @@
         def _():
             sum_ref[...] += product
 
-        if kind == "second":
+        if kind == "last":
 
             @pl.when(step == steps // 2 - 1)
             def _():
@@ -165,7 +170,9 @@
     hidden_width = w1.shape[1]
     steps = 6
     block = hidden_width // steps
-    shift = steps // 2 if kind == "second" else 0
+    half_steps = steps // 2
+    shift = {"first": 0, "middle": half_steps - 1, "last": half_steps, "far": 0}[kind]
+    count = {"first": half_steps - 1, "middle": 1, "last": half_steps, "far": steps}[kind]
 
     def column(i, h):
         return (0, (i + shift + h[2] * (steps // 2)) % steps)
@@ -174,7 +181,7 @@
         return ((i + shift + h[2] * (steps // 2)) % steps, 0)
 
     def held(i, h):
-        return (0, jnp.minimum(i, steps // 2 - 1))
+        return (0, jnp.minimum(i + shift, steps // 2 - 1))
 
     def whole(i, h):
         return (0, 0)
@@ -199,7 +206,13 @@
         out_specs = [gi_spec, go_spec, whole_spec]
         out_shape = [gi_shape, go_shape, sum_shape]
         scratch = [xt, ut]
-    elif kind == "second":
+    elif kind == "middle":
+        in_specs += [whole_spec] + [pl.BlockSpec(memory_space=pl.ANY)] * 2
+        out_specs = [gi_spec, go_spec, whole_spec]
+        out_shape = [gi_shape, go_shape, sum_shape]
+        scratch = [xt]
+        aliases = {6: 0, 7: 1}
+    elif kind == "last":
         in_specs += [whole_spec, pl.BlockSpec(memory_space=pl.ANY)]
         out_specs = [gi_spec, whole_spec]
         out_shape = [gi_shape, jax.ShapeDtypeStruct((rows, width), bf16)]
@@ -214,7 +227,7 @@
         functools.partial(expert_kernel, steps=steps, kind=kind),
         grid_spec=pltpu.PrefetchScalarGridSpec(
             num_scalar_prefetch=1,
-            grid=(steps if kind == "far" else steps // 2,),
+            grid=(count,),
             in_specs=in_specs,
             out_specs=out_specs,
             scratch_shapes=scratch,
@@ -422,11 +435,9 @@
         "first", info, after(inputs, upstream), upstream, w_first, w_second
     )
     far_scaled = after(far_scaled, partial_out)
-    far_upstream = dispatch(far_table, far_scaled, experts)[0]
-    far_tokens = after(far_tokens, partial_out)
-    far_inputs, far_sent = dispatch(far_table, far_tokens, experts)
-    own_in, expert_out = expert_call(
-        "second",
+    far_upstream, far_sent = dispatch(far_table, far_scaled, experts)
+    own_in, own_out, partial_out = expert_call(
+        "middle",
         info,
         inputs,
         upstream,
@@ -434,9 +445,22 @@
         w_second,
         after(partial_out, *far_sent),
         own_in,
-    )
-
-    expert_out = after(expert_out, far_upstream)
+        own_out,
+    )
+    far_tokens = after(far_tokens, partial_out)
+    far_inputs, far_sent = dispatch(far_table, far_tokens, experts)
+    own_in, expert_out = expert_call(
+        "last",
+        info,
+        inputs,
+        upstream,
+        w_first,
+        w_second,
+        after(partial_out, *far_sent),
+        own_in,
+    )
+
+    expert_out = after(expert_out, far_upstream, far_inputs)
     returned = exchange_blocks(
         [expert_out[j * capacity : (j + 1) * capacity] for j in range(experts)]
     )
@@ -456,19 +480,21 @@
     scale = 16384.0 * lax.rsqrt(jnp.maximum(norm, 1e-12))
     weight_own, weight_far = coef_own * scale, coef_far * scale
 
-    def quarter(own, far, other, axis):
+    def quarter(own, far, other, axis, left, right):
         size = own.shape[axis] // top
         own, far = (
             lax.dynamic_slice_in_dim(x, (member ^ other) * size, size, axis) for x in (own, far)
         )
-        return weight_own[0] * own + weight_far[0] * far
+        return left * own + right * far
 
     def exchange(own, far, axis):
-        received = [quarter(own, far, 0, axis)]
-        for other in range(1, top):
-            outgoing = quarter(own, far, other, axis).astype(f16)
-            received.append(swap(outgoing, "dp", other).astype(f32))
-        return received
+        pair = (weight_own[0], weight_far[0])
+        others = range(1, top)
+        outgoing = [quarter(own, far, other, axis, *pair).astype(f16) for other in others]
+        if axis == 0:
+            pair = [after(weight, *outgoing) for weight in pair]
+        received = [swap(x, "dp", other).astype(f32) for x, other in zip(outgoing, others)]
+        return [quarter(own, far, 0, axis, *pair)] + received
 
     firsts = exchange(own_in, far_in, 0)
     seconds = exchange(own_out, far_out, 1)

time: 216 us -> 212 us (0.981)
  waiting for transfers between devices: 73.6 us -> 68.8 us
  Pallas kernels: 69.6 us -> 73.1 us
  local copies, waits for them, and re-layouts: 6.79 us -> 4.32 us
    ppermute x28, waiting for transfers between devices: 73.6 us -> 68.8 us  [swap(): lax.ppermute(x, axis, [(i, i ^ offset) for i in range(lax.axis_size(axis))])]
    pallas_call x3 -> x4, Pallas kernels: 58.9 us -> 62.9 us  [expert_call(): pl.pallas_call(functools.partial(expert_kernel, steps=steps, kind=kind),...]
  transfers between devices with their start and end apart: 28 -> 28, of which waited for: 12 -> 12; matrix products, arithmetic and copies ran while one was open for 13% -> 13% of each run, Pallas kernels for 28% -> 31%
where the time goes in v2:
time: 212 us; the launch traced here: 211 us
  Pallas kernels  73.1 us (34%)
  waiting for transfers between devices  68.8 us (32%)
  starting transfers between devices  35.2 us (17%)
  other arithmetic  20.1 us (9%)
  matrix products  8.51 us (4%)
  local copies, waits for them, and re-layouts  4.32 us (2%)
    ppermute x28, waiting for transfers between devices, swap(): lax.ppermute(x, axis, [(i, i ^ offset) for i in range(lax.axis_size(axis))])  68.8 us
    pallas_call x4, Pallas kernels, expert_call(): pl.pallas_call(functools.partial(expert_kernel, steps=steps, kind=kind),...  62.9 us
    ppermute x28, starting transfers between devices, swap(): lax.ppermute(x, axis, [(i, i ^ offset) for i in range(lax.axis_size(axis))])  35.2 us
    convert_element_type x2, other arithmetic, exchange(): quarter(own, far, other, axis, *pair).astype(f16)  8.32 us
    dot_general x4, matrix products, place_rows(): sent = jnp.dot(table, rows, preferred_element_type=f32).astype(bf16)  6.38 us
    pallas_call x1, Pallas kernels, update_call(): pl.pallas_call(functools.partial(update_kernel, count=count), grid_spec=p...  6.09 us
    another operation x4, other arithmetic  5.09 us
  transfers between devices with their start and end apart: 28, of which 12 were waited for; matrix products, arithmetic and copies ran while one was open for 13% of the time, Pallas kernels for 31%

profile of v2, /device:TPU:0, one launch (start us, length us, event | category | flops | bytes accessed | tf_op | source)
XLA Modules:
  0.0 211.3 jit_solution(13596774176772140527)
XLA Ops:
  0.6 4.1 %collective-permute-start.6 = (s32[4,128]{1,0:T(4,128)}, s32[4,128]{1,0:T(4,128)S(1)}, u32[]{:S(2)}, u32[]{:S(2)}) collective-permute-start(s32[4,128]{1,0:T(4,128)} %bitcast.118), channel_id=1, source_target_pairs={{0,16},{4,20},{8,24},{12,28},{16,0},{20,4},{24,8},{28,12},{1,17},{... | collective-permute-start | bytes 6152 | tf_op jit(solution)/shard_map/ppermute | solution.py:25
  11.8 2.2 %fusion.6 = bf16[1024,768]{1,0:T(8,128)(2,1)S(1)} fusion(bf16[512,768]{1,0:T(8,128)(2,1)} %param.10, s32[512]{0:T(512)S(1)} %multiply_add_fusion.3), kind=kOutput, calls=%fused_computation.8 | convolution fusion | flops 806617088 | bytes 2361344 | tf_op jit(solution)/shard_map/dot_general | solution.py:69
  15.9 2.3 %reduce-window.16 = s32[4,4,128]{2,1,0:T(4,128)S(1)} reduce-window(s32[4,4,128]{2,1,0:T(4,128)} %fusion.30, s32[]{:T(128)} %constant.48.clone.1), window={size=1x1x128 pad=0_0x0_0x127_0}, to_apply=%region_3.4 | reduce-window | flops 260096 | bytes 16388 | tf_op jit(solution)/shard_map/reduce-window.2
  22.9 6.5 %collective-permute-done.5 = bf16[256,768]{1,0:T(8,128)(2,1)S(1)} collective-permute-done((bf16[256,768]{1,0:T(8,128)(2,1)S(1)}, bf16[256,768]{1,0:T(8,128)(2,1)S(1)}, u32[]{:S(2)}, u32[]{:S(2)}) %collective-permute-start.5) | collective-permute-done | bytes 393248 | tf_op jit(solution)/shard_map/ppermute | solution.py:25
  29.6 2.9 %collective-permute-start.8 = (bf16[512,768]{1,0:T(8,128)(2,1)S(1)}, bf16[512,768]{1,0:T(8,128)(2,1)S(1)}, u32[]{:S(2)}, u32[]{:S(2)}) collective-permute-start(bf16[512,768]{1,0:T(8,128)(2,1)S(1)} %copy-done.8), channel_id=1, source_target_pairs={{0,16},{4,20},{8,24},{12,28},{16,0},{20,4},{24,8},{28,12},{1,17},{... | collective-permute-start | bytes 2359304 | tf_op jit(solution)/shard_map/ppermute | solution.py:25
  32.5 6.1 %collective-permute-done.1 = bf16[256,768]{1,0:T(8,128)(2,1)S(1)} collective-permute-done((bf16[256,768]{1,0:T(8,128)(2,1)}, bf16[256,768]{1,0:T(8,128)(2,1)S(1)}, u32[]{:S(2)}, u32[]{:S(2)}) %collective-permute-start.1) | collective-permute-done | bytes 393248 | tf_op jit(solution)/shard_map/ppermute | solution.py:25
  38.6 7.7 %collective-permute-done.2 = bf16[256,768]{1,0:T(8,128)(2,1)S(1)} collective-permute-done((bf16[256,768]{1,0:T(8,128)(2,1)}, bf16[256,768]{1,0:T(8,128)(2,1)S(1)}, u32[]{:S(2)}, u32[]{:S(2)}) %collective-permute-start.2) | collective-permute-done | bytes 393248 | tf_op jit(solution)/shard_map/ppermute | solution.py:25
  47.4 13.6 %shard_map.153 = (f32[384,3072]{1,0:T(8,128)}, f32[768,1536]{1,0:T(8,128)}, f32[1024,768]{1,0:T(8,128)}) custom-call(s32[3]{0:T(128)S(1)} %pad_add_fusion.info_ref, bf16[1024,768]{1,0:T(8,128)(2,1)S(1)} %pad_maximum_fusion.x_ref, bf16[1024,768]{1,0:T(8,128)(2,1)S(1)} %pad_maximum_fusion.1.u_ref, bf16[768,3072]{1,0:T(8,128)(2,1)} %bitcast.106, ...), custom_call_target="tpu_custom_call" | custom-call | flops 1024 | bytes 1024 | tf_op jit(solution)/shard_map/pallas_call | solution.py:226
  61.1 2.2 %fusion.7 = bf16[1024,768]{1,0:T(8,128)(2,1)S(1)} fusion(bf16[512,768]{1,0:T(8,128)(2,1)} %collective-permute-done.7, s32[512]{0:T(512)S(1)} %multiply_add_fusion.2), kind=kOutput, calls=%fused_computation.9 | convolution fusion | flops 806617088 | bytes 2361344 | tf_op jit(solution)/shard_map/dot_general | solution.py:69
  65.6 9.0 %shard_map.154 = (f32[384,3072]{1,0:T(8,128)}, f32[768,1536]{1,0:T(8,128)}, f32[1024,768]{1,0:T(8,128)}) custom-call(s32[3]{0:T(128)S(1)} %pad_add_fusion.info_ref, bf16[1024,768]{1,0:T(8,128)(2,1)S(1)} %pad_maximum_fusion.x_ref, bf16[1024,768]{1,0:T(8,128)(2,1)S(1)} %pad_maximum_fusion.1.u_ref, ...), custom_call_target="tpu_custom_call", output_to_operand_aliasing={{0}: (6, {}), {1}: (7, {})} | custom-call | flops 1024 | bytes 1024 | tf_op jit(solution)/shard_map/pallas_call | solution.py:226
  74.6 2.1 collective-permute-done.8
  79.7 14.9 %shard_map.155 = (f32[384,3072]{1,0:T(8,128)}, bf16[1024,768]{1,0:T(8,128)(2,1)S(1)}) custom-call(s32[3]{0:T(128)S(1)} %pad_add_fusion.info_ref, bf16[1024,768]{1,0:T(8,128)(2,1)S(1)} %pad_maximum_fusion.x_ref, bf16[1024,768]{1,0:T(8,128)(2,1)S(1)} %pad_maximum_fusion.1.u_ref, bf16[768,3072]{1,0:T(8,128)(2,1)} %bitcast.108, ...), custom_call_target="tpu_custom_call", output_to_operand_aliasing={{0}: (6, {})} | custom-call | flops 1024 | bytes 1024 | tf_op jit(solution)/shard_map/pallas_call | solution.py:226
  94.7 5.2 %collective-permute-done.14 = bf16[256,768]{1,0:T(8,128)(2,1)S(1)} collective-permute-done((bf16[256,768]{1,0:T(8,128)(2,1)S(1)}, bf16[256,768]{1,0:T(8,128)(2,1)S(1)}, u32[]{:S(2)}, u32[]{:S(2)}) %collective-permute-start.14) | collective-permute-done | bytes 393248 | tf_op jit(solution)/shard_map/ppermute | solution.py:25
  102.2 25.4 %shard_map.156 = (f32[384,3072]{1,0:T(8,128)}, f32[768,1536]{1,0:T(8,128)}, f32[8,128]{1,0:T(8,128)S(1)}) custom-call(s32[3]{0:T(128)S(1)} %pad_add_fusion.info_ref, bf16[1024,768]{1,0:T(8,128)(2,1)S(1)} %pad_maximum_fusion.3.x_ref, bf16[1024,768]{1,0:T(8,128)(2,1)S(1)} %pad_maximum_fusion.2.u_ref, bf16[768,3072]{1,0:T(8,128)(2,1)} %bitcast.109, ...), custom_call_target="tpu_custom_call" | custom-call | flops 1024 | bytes 1024 | tf_op jit(solution)/shard_map/pallas_call | solution.py:226
  128.5 2.7 %collective-permute-start.18 = (f32[8,128]{1,0:T(8,128)S(1)}, f32[8,128]{1,0:T(8,128)S(1)}, u32[]{:S(2)}, u32[]{:S(2)}) collective-permute-start(f32[8,128]{1,0:T(8,128)S(1)} %get-tuple-element.54), channel_id=1, source_target_pairs={{0,16},{4,20},{8,24},{12,28},{16,0},{20,4},{24,8},{28,12},{1,17},{... | collective-permute-start | bytes 12296 | tf_op jit(solution)/shard_map/ppermute | solution.py:25
  131.2 1.8 collective-permute-done.18
  133.0 3.9 %add_convert_fusion.3 = (f16[96,3072]{1,0:T(8,128)(2,1)S(1)}, f16[96,3072]{1,0:T(8,128)(2,1)S(1)}, f16[96,3072]{1,0:T(8,128)(2,1)S(1)}) fusion(f32[384,3072]{1,0:T(8,128)} %get-tuple-element.55, s32[]{:T(128)S(6)} %select_n.47, f32[384,3072]{1,0:T(8,128)} %get-tuple-element.51.rest_0_, f32[]{:T(128)S(1)} %bitcast.128, f32[]{:T(128)S(1)} %bitcast.123, ...), kind=kLoop, calls=%fused_computation.29 | loop fusion | flops 3538944 | bytes 8847380 | tf_op jit(solution)/shard_map/convert_element_type | solution.py:493
  136.9 1.8 collective-permute-start.19
  140.4 4.5 %add_convert_fusion = (f16[768,384]{1,0:T(8,128)(2,1)S(1)}, f16[768,384]{1,0:T(8,128)(2,1)S(1)}, f16[768,384]{1,0:T(8,128)(2,1)S(1)}, f32[768,384]{1,0:T(8,128)S(1)}) fusion(f32[768,1536]{1,0:T(8,128)} %get-tuple-element.58, s32[]{:T(128)S(6)} %select_n.52, f32[768,1536]{1,0:T(8,128)} %get-tuple-element.52.rest_1_, f32[]{:T(128)S(1)} %bitcast.129, ...), kind=kLoop, calls=%fused_computation.24 | loop fusion | flops 4423680 | bytes 12386328 | tf_op jit(solution)/shard_map/convert_element_type | solution.py:493
  144.9 1.8 collective-permute-start.22
  148.1 16.3 %collective-permute-done.19 = f16[96,3072]{1,0:T(8,128)(2,1)S(1)} collective-permute-done((f16[96,3072]{1,0:T(8,128)(2,1)S(1)}, f16[96,3072]{1,0:T(8,128)(2,1)S(1)}, u32[]{:S(2)}, u32[]{:S(2)}) %collective-permute-start.19) | collective-permute-done | bytes 589856 | tf_op jit(solution)/shard_map/ppermute | solution.py:25
  164.3 2.5 %collective-permute-start.24 = (f16[768,384]{1,0:T(8,128)(2,1)S(1)}, f16[768,384]{1,0:T(8,128)(2,1)S(1)}, u32[]{:S(2)}, u32[]{:S(2)}) collective-permute-start(f16[768,384]{1,0:T(8,128)(2,1)S(1)} %get-tuple-element.70), channel_id=1, source_target_pairs={{0,12},{4,8},{8,4},{12,0},{16,28},{20,24},{24,20},{28,16},{1,13},{... | collective-permute-start | bytes 1769480 | tf_op jit(solution)/shard_map/ppermute | solution.py:25
  166.9 1.8 multiply_add_fusion.1.refs_0_
  169.0 2.4 %shard_map.157.before_ref = f32[8,128]{1,0:T(8,128)S(1)} custom-call(s32[3]{0:T(128)S(1)} %pad_add_fusion.info_ref, f32[1,128]{1,0:T(1,128)S(1)} %rsqrt_multiply_fusion.1.before_ref, f32[96,3072]{1,0:T(8,128)S(1)} %multiply_add_fusion.1.refs_0_, f32[96,3072]{1,0:T(8,128)S(1)} %convert_element_type.87.refs_1_, f32[96,3072]{1,0:T(8,128)S(1)} %convert_element_type.88.refs_2_, ...), custom_call_target="tpu_custom_call" | custom-call | tf_op jit(solution)/shard_map/pallas_call | solution.py:282
  171.4 6.1 %collective-permute-done.22 = f16[768,384]{1,0:T(8,128)(2,1)S(1)} collective-permute-done((f16[768,384]{1,0:T(8,128)(2,1)S(1)}, f16[768,384]{1,0:T(8,128)(2,1)S(1)}, u32[]{:S(2)}, u32[]{:S(2)}) %collective-permute-start.22) | collective-permute-done | bytes 589856 | tf_op jit(solution)/shard_map/ppermute | solution.py:25
  177.6 2.7 %collective-permute-done.23 = f16[768,384]{1,0:T(8,128)(2,1)S(1)} collective-permute-done((f16[768,384]{1,0:T(8,128)(2,1)S(1)}, f16[768,384]{1,0:T(8,128)(2,1)S(1)}, u32[]{:S(2)}, u32[]{:S(2)}) %collective-permute-start.23) | collective-permute-done | bytes 589856 | tf_op jit(solution)/shard_map/ppermute | solution.py:25
  180.3 10.4 %collective-permute-done.24 = f16[768,384]{1,0:T(8,128)(2,1)S(1)} collective-permute-done((f16[768,384]{1,0:T(8,128)(2,1)S(1)}, f16[768,384]{1,0:T(8,128)(2,1)S(1)}, u32[]{:S(2)}, u32[]{:S(2)}) %collective-permute-start.24) | collective-permute-done | bytes 589856 | tf_op jit(solution)/shard_map/ppermute | solution.py:25
  194.3 2.0 collective-permute-done.25
  198.1 1.9 collective-permute-done.26
  199.9 2.7 %collective-permute-start.27 = (f32[8,128]{1,0:T(8,128)S(1)}, f32[8,128]{1,0:T(8,128)S(1)}, u32[]{:S(2)}, u32[]{:S(2)}) collective-permute-start(f32[8,128]{1,0:T(8,128)S(1)} %add.160.mine_ref), channel_id=1, source_target_pairs={{0,16},{4,20},{8,24},{12,28},{16,0},{20,4},{24,8},{28,12},{1,17},{... | collective-permute-start | bytes 12296 | tf_op jit(solution)/shard_map/ppermute | solution.py:25
  202.7 2.1 %multiply_convert_fusion = bf16[512,768]{1,0:T(8,128)(2,1)} fusion(bf16[256,768]{1,0:T(8,128)(2,1)S(1)} %copy-done.12, bf16[256,768]{1,0:T(8,128)(2,1)S(1)} %copy-done.10, bf16[256,768]{1,0:T(8,128)(2,1)S(1)} %collective-permute-done.15, bf16[256,768]{1,0:T(8,128)(2,1)S(1)} %get-tuple-element.77, s32[512]{0:T(512)S(1)} %copy-done.7, f32[512]{0:T(512)S(1)} %bitcast.132), kind=kOutput, calls=%fused_computation.22 | convolution fusion | flops 812908544 | bytes 2363392 | tf_op jit(solution)/shard_map/dot_general | solution.py:47
  205.0 6.1 %shard_map.159 = (f32[1,96,3072]{2,1,0:T(8,128)}, f32[1,384,768]{2,1,0:T(8,128)}, f32[1,96,3072]{2,1,0:T(8,128)}, f32[1,384,768]{2,1,0:T(8,128)}, f32[1,96,3072]{2,1,0:T(8,128)}, /*index=5*/f32[1,384,768]{2,1,0:T(8,128)}) custom-call(s32[3]{0:T(128)S(1)} %pad_add_fusion.info_ref, f32[8,128]{1,0:T(8,128)S(1)} %add.160.mine_ref, ...), custom_call_target="tpu_custom_call" | custom-call | tf_op jit(solution)/shard_map/pallas_call | solution.py:367
  (112 shorter events, 32.6 us)
Async XLA Ops:
  0.6 14.4 %collective-permute-start.6 = (s32[4,128]{1,0:T(4,128)}, s32[4,128]{1,0:T(4,128)S(1)}, u32[]{:S(2)}, u32[]{:S(2)}) collective-permute-start(s32[4,128]{1,0:T(4,128)} %bitcast.118), channel_id=1, source_target_pairs={{0,16},{4,20},{8,24},{12,28},{16,0},{20,4},{24,8},{28,12},{1,17},{... | collective-permute-start | bytes 6152 | tf_op jit(solution)/shard_map/ppermute | solution.py:25
  6.1 55.0 %collective-permute-start.7 = (bf16[512,768]{1,0:T(8,128)(2,1)S(1)}, bf16[512,768]{1,0:T(8,128)(2,1)}, u32[]{:S(2)}, u32[]{:S(2)}) collective-permute-start(bf16[512,768]{1,0:T(8,128)(2,1)S(1)} %multiply_convert_fusion.1), channel_id=1, source_target_pairs={{0,16},{4,20},{8,24},{12,28},{16,0},{20,4},{24,8},{28,12},{1,17},{... | collective-permute-start | bytes 2359304 | tf_op jit(solution)/shard_map/ppermute | solution.py:25
  9.8 11.3 %collective-permute-start.3 = (bf16[256,768]{1,0:T(8,128)(2,1)}, bf16[256,768]{1,0:T(8,128)(2,1)S(1)}, u32[]{:S(2)}, u32[]{:S(2)}) collective-permute-start(bf16[256,768]{1,0:T(8,128)(2,1)} %get-tuple-element.95), channel_id=1, source_target_pairs={{0,1},{1,0},{2,3},{3,2},{4,5},{5,4},{6,7},{7,6},{8,9},{9,8},{10,11... | collective-permute-start | bytes 1179656 | tf_op jit(solution)/shard_map/ppermute | solution.py:25
  9.8 13.1 %collective-permute-start.4 = (bf16[256,768]{1,0:T(8,128)(2,1)S(1)}, bf16[256,768]{1,0:T(8,128)(2,1)S(1)}, u32[]{:S(2)}, u32[]{:S(2)}) collective-permute-start(bf16[256,768]{1,0:T(8,128)(2,1)S(1)} %get-tuple-element.94), channel_id=1, source_target_pairs={{0,2},{1,3},{2,0},{3,1},{4,6},{5,7},{6,4},{7,5},{8,10},{9,11},{10,... | collective-permute-start | bytes 1179656 | tf_op jit(solution)/shard_map/ppermute | solution.py:25
  11.6 17.9 %collective-permute-start.5 = (bf16[256,768]{1,0:T(8,128)(2,1)S(1)}, bf16[256,768]{1,0:T(8,128)(2,1)S(1)}, u32[]{:S(2)}, u32[]{:S(2)}) collective-permute-start(bf16[256,768]{1,0:T(8,128)(2,1)S(1)} %get-tuple-element.93), channel_id=1, source_target_pairs={{0,3},{1,2},{2,1},{3,0},{4,7},{5,6},{6,5},{7,4},{8,11},{9,10},{10,... | collective-permute-start | bytes 1179656 | tf_op jit(solution)/shard_map/ppermute | solution.py:25
  15.0 17.4 %collective-permute-start = (bf16[256,768]{1,0:T(8,128)(2,1)}, bf16[256,768]{1,0:T(8,128)(2,1)}, u32[]{:S(2)}, u32[]{:S(2)}) collective-permute-start(bf16[256,768]{1,0:T(8,128)(2,1)} %get-tuple-element.92), channel_id=1, source_target_pairs={{0,1},{1,0},{2,3},{3,2},{4,5},{5,4},{6,7},{7,6},{8,9},{9,8},{10,11... | collective-permute-start | bytes 1179656 | tf_op jit(solution)/shard_map/ppermute | solution.py:25
  21.1 17.5 %collective-permute-start.1 = (bf16[256,768]{1,0:T(8,128)(2,1)}, bf16[256,768]{1,0:T(8,128)(2,1)S(1)}, u32[]{:S(2)}, u32[]{:S(2)}) collective-permute-start(bf16[256,768]{1,0:T(8,128)(2,1)} %get-tuple-element.91), channel_id=1, source_target_pairs={{0,2},{1,3},{2,0},{3,1},{4,6},{5,7},{6,4},{7,5},{8,10},{9,11},{10,... | collective-permute-start | bytes 1179656 | tf_op jit(solution)/shard_map/ppermute | solution.py:25
  22.9 23.4 %collective-permute-start.2 = (bf16[256,768]{1,0:T(8,128)(2,1)}, bf16[256,768]{1,0:T(8,128)(2,1)S(1)}, u32[]{:S(2)}, u32[]{:S(2)}) collective-permute-start(bf16[256,768]{1,0:T(8,128)(2,1)} %get-tuple-element.90), channel_id=1, source_target_pairs={{0,3},{1,2},{2,1},{3,0},{4,7},{5,6},{6,5},{7,4},{8,11},{9,10},{10,... | collective-permute-start | bytes 1179656 | tf_op jit(solution)/shard_map/ppermute | solution.py:25
  29.6 47.0 %collective-permute-start.8 = (bf16[512,768]{1,0:T(8,128)(2,1)S(1)}, bf16[512,768]{1,0:T(8,128)(2,1)S(1)}, u32[]{:S(2)}, u32[]{:S(2)}) collective-permute-start(bf16[512,768]{1,0:T(8,128)(2,1)S(1)} %copy-done.8), channel_id=1, source_target_pairs={{0,16},{4,20},{8,24},{12,28},{16,0},{20,4},{24,8},{28,12},{1,17},{... | collective-permute-start | bytes 2359304 | tf_op jit(solution)/shard_map/ppermute | solution.py:25
  63.3 16.0 %collective-permute-start.10 = (bf16[256,768]{1,0:T(8,128)(2,1)S(1)}, bf16[256,768]{1,0:T(8,128)(2,1)S(1)}, u32[]{:S(2)}, u32[]{:S(2)}) collective-permute-start(bf16[256,768]{1,0:T(8,128)(2,1)S(1)} %get-tuple-element.86), channel_id=1, source_target_pairs={{0,2},{1,3},{2,0},{3,1},{4,6},{5,7},{6,4},{7,5},{8,10},{9,11},{10,... | collective-permute-start | bytes 1179656 | tf_op jit(solution)/shard_map/ppermute | solution.py:25
  65.1 29.5 %collective-permute-start.11 = (bf16[256,768]{1,0:T(8,128)(2,1)S(1)}, bf16[256,768]{1,0:T(8,128)(2,1)S(1)}, u32[]{:S(2)}, u32[]{:S(2)}) collective-permute-start(bf16[256,768]{1,0:T(8,128)(2,1)S(1)} %get-tuple-element.85), channel_id=1, source_target_pairs={{0,3},{1,2},{2,1},{3,0},{4,7},{5,6},{6,5},{7,4},{8,11},{9,10},{10,... | collective-permute-start | bytes 1179656 | tf_op jit(solution)/shard_map/ppermute | solution.py:25
  65.4 29.2 %collective-permute-start.9 = (bf16[256,768]{1,0:T(8,128)(2,1)S(1)}, bf16[256,768]{1,0:T(8,128)(2,1)S(1)}, u32[]{:S(2)}, u32[]{:S(2)}) collective-permute-start(bf16[256,768]{1,0:T(8,128)(2,1)S(1)} %get-tuple-element.87), channel_id=1, source_target_pairs={{0,1},{1,0},{2,3},{3,2},{4,5},{5,4},{6,7},{7,6},{8,9},{9,8},{10,11... | collective-permute-start | bytes 1179656 | tf_op jit(solution)/shard_map/ppermute | solution.py:25
  77.8 17.0 %collective-permute-start.12 = (bf16[256,768]{1,0:T(8,128)(2,1)S(1)}, bf16[256,768]{1,0:T(8,128)(2,1)S(1)}, u32[]{:S(2)}, u32[]{:S(2)}) collective-permute-start(bf16[256,768]{1,0:T(8,128)(2,1)S(1)} %get-tuple-element.83), channel_id=1, source_target_pairs={{0,1},{1,0},{2,3},{3,2},{4,5},{5,4},{6,7},{7,6},{8,9},{9,8},{10,11... | collective-permute-start | bytes 1179656 | tf_op jit(solution)/shard_map/ppermute | solution.py:25
  77.8 16.9 %collective-permute-start.13 = (bf16[256,768]{1,0:T(8,128)(2,1)S(1)}, bf16[256,768]{1,0:T(8,128)(2,1)S(1)}, u32[]{:S(2)}, u32[]{:S(2)}) collective-permute-start(bf16[256,768]{1,0:T(8,128)(2,1)S(1)} %get-tuple-element.82), channel_id=1, source_target_pairs={{0,2},{1,3},{2,0},{3,1},{4,6},{5,7},{6,4},{7,5},{8,10},{9,11},{10,... | collective-permute-start | bytes 1179656 | tf_op jit(solution)/shard_map/ppermute | solution.py:25
  79.4 20.6 %collective-permute-start.14 = (bf16[256,768]{1,0:T(8,128)(2,1)S(1)}, bf16[256,768]{1,0:T(8,128)(2,1)S(1)}, u32[]{:S(2)}, u32[]{:S(2)}) collective-permute-start(bf16[256,768]{1,0:T(8,128)(2,1)S(1)} %get-tuple-element.81), channel_id=1, source_target_pairs={{0,3},{1,2},{2,1},{3,0},{4,7},{5,6},{6,5},{7,4},{8,11},{9,10},{10,... | collective-permute-start | bytes 1179656 | tf_op jit(solution)/shard_map/ppermute | solution.py:25
  100.2 27.4 %collective-permute-start.15 = (bf16[256,768]{1,0:T(8,128)(2,1)S(1)}, bf16[256,768]{1,0:T(8,128)(2,1)S(1)}, u32[]{:S(2)}, u32[]{:S(2)}) collective-permute-start(bf16[256,768]{1,0:T(8,128)(2,1)S(1)} %get-tuple-element.80), channel_id=1, source_target_pairs={{0,1},{1,0},{2,3},{3,2},{4,5},{5,4},{6,7},{7,6},{8,9},{9,8},{10,11... | collective-permute-start | bytes 1179656 | tf_op jit(solution)/shard_map/ppermute | solution.py:25
  100.4 27.2 %collective-permute-start.16 = (bf16[256,768]{1,0:T(8,128)(2,1)S(1)}, bf16[256,768]{1,0:T(8,128)(2,1)S(1)}, u32[]{:S(2)}, u32[]{:S(2)}) collective-permute-start(bf16[256,768]{1,0:T(8,128)(2,1)S(1)} %get-tuple-element.79), channel_id=1, source_target_pairs={{0,2},{1,3},{2,0},{3,1},{4,6},{5,7},{6,4},{7,5},{8,10},{9,11},{10,... | collective-permute-start | bytes 1179656 | tf_op jit(solution)/shard_map/ppermute | solution.py:25
  102.2 25.4 %collective-permute-start.17 = (bf16[256,768]{1,0:T(8,128)(2,1)S(1)}, bf16[256,768]{1,0:T(8,128)(2,1)S(1)}, u32[]{:S(2)}, u32[]{:S(2)}) collective-permute-start(bf16[256,768]{1,0:T(8,128)(2,1)S(1)} %get-tuple-element.78), channel_id=1, source_target_pairs={{0,3},{1,2},{2,1},{3,0},{4,7},{5,6},{6,5},{7,4},{8,11},{9,10},{10,... | collective-permute-start | bytes 1179656 | tf_op jit(solution)/shard_map/ppermute | solution.py:25
  128.5 4.5 %collective-permute-start.18 = (f32[8,128]{1,0:T(8,128)S(1)}, f32[8,128]{1,0:T(8,128)S(1)}, u32[]{:S(2)}, u32[]{:S(2)}) collective-permute-start(f32[8,128]{1,0:T(8,128)S(1)} %get-tuple-element.54), channel_id=1, source_target_pairs={{0,16},{4,20},{8,24},{12,28},{16,0},{20,4},{24,8},{28,12},{1,17},{... | collective-permute-start | bytes 12296 | tf_op jit(solution)/shard_map/ppermute | solution.py:25
  136.9 27.5 %collective-permute-start.19 = (f16[96,3072]{1,0:T(8,128)(2,1)S(1)}, f16[96,3072]{1,0:T(8,128)(2,1)S(1)}, u32[]{:S(2)}, u32[]{:S(2)}) collective-permute-start(f16[96,3072]{1,0:T(8,128)(2,1)S(1)} %get-tuple-element.76), channel_id=1, source_target_pairs={{0,4},{4,0},{8,12},{12,8},{16,20},{20,16},{24,28},{28,24},{1,5},{5... | collective-permute-start | bytes 1769480 | tf_op jit(solution)/shard_map/ppermute | solution.py:25
  138.7 30.1 %collective-permute-start.20 = (f16[96,3072]{1,0:T(8,128)(2,1)S(1)}, f16[96,3072]{1,0:T(8,128)(2,1)S(1)}, u32[]{:S(2)}, u32[]{:S(2)}) collective-permute-start(f16[96,3072]{1,0:T(8,128)(2,1)S(1)} %get-tuple-element.75), channel_id=1, source_target_pairs={{0,8},{4,12},{8,0},{12,4},{16,24},{20,28},{24,16},{28,20},{1,9},{5... | collective-permute-start | bytes 1769480 | tf_op jit(solution)/shard_map/ppermute | solution.py:25
  140.1 28.8 %collective-permute-start.21 = (f16[96,3072]{1,0:T(8,128)(2,1)S(1)}, f16[96,3072]{1,0:T(8,128)(2,1)S(1)}, u32[]{:S(2)}, u32[]{:S(2)}) collective-permute-start(f16[96,3072]{1,0:T(8,128)(2,1)S(1)} %get-tuple-element.74), channel_id=1, source_target_pairs={{0,12},{4,8},{8,4},{12,0},{16,28},{20,24},{24,20},{28,16},{1,13},{... | collective-permute-start | bytes 1769480 | tf_op jit(solution)/shard_map/ppermute | solution.py:25
  144.9 32.6 %collective-permute-start.22 = (f16[768,384]{1,0:T(8,128)(2,1)S(1)}, f16[768,384]{1,0:T(8,128)(2,1)S(1)}, u32[]{:S(2)}, u32[]{:S(2)}) collective-permute-start(f16[768,384]{1,0:T(8,128)(2,1)S(1)} %get-tuple-element.72), channel_id=1, source_target_pairs={{0,4},{4,0},{8,12},{12,8},{16,20},{20,16},{24,28},{28,24},{1,5},{5... | collective-permute-start | bytes 1769480 | tf_op jit(solution)/shard_map/ppermute | solution.py:25
  146.7 33.6 %collective-permute-start.23 = (f16[768,384]{1,0:T(8,128)(2,1)S(1)}, f16[768,384]{1,0:T(8,128)(2,1)S(1)}, u32[]{:S(2)}, u32[]{:S(2)}) collective-permute-start(f16[768,384]{1,0:T(8,128)(2,1)S(1)} %get-tuple-element.71), channel_id=1, source_target_pairs={{0,8},{4,12},{8,0},{12,4},{16,24},{20,28},{24,16},{28,20},{1,9},{5... | collective-permute-start | bytes 1769480 | tf_op jit(solution)/shard_map/ppermute | solution.py:25
  164.3 26.4 %collective-permute-start.24 = (f16[768,384]{1,0:T(8,128)(2,1)S(1)}, f16[768,384]{1,0:T(8,128)(2,1)S(1)}, u32[]{:S(2)}, u32[]{:S(2)}) collective-permute-start(f16[768,384]{1,0:T(8,128)(2,1)S(1)} %get-tuple-element.70), channel_id=1, source_target_pairs={{0,12},{4,8},{8,4},{12,0},{16,28},{20,24},{24,20},{28,16},{1,13},{... | collective-permute-start | bytes 1769480 | tf_op jit(solution)/shard_map/ppermute | solution.py:25
  180.3 24.5 %copy-start.3 = (f32[1,384,768]{2,1,0:T(8,128)S(1)}, f32[1,384,768]{2,1,0:T(8,128)}, u32[]{:S(2)}) copy-start(f32[1,384,768]{2,1,0:T(8,128)} %refs_13_.1) | copy-start | bytes 3538948
  190.7 11.8 %copy-start.12 = (bf16[256,768]{1,0:T(8,128)(2,1)S(1)}, bf16[256,768]{1,0:T(8,128)(2,1)}, u32[]{:S(2)}) copy-start(bf16[256,768]{1,0:T(8,128)(2,1)} %copy-done.11) | copy-start | bytes 1179652
  190.8 14.0 %slice-start = ((s8[4718592]{0:T(1024)(128)(4,1)}), s8[4194304]{0:T(1024)(128)(4,1)S(1)}, s32[]{:S(2)}) async-start(s8[4718592]{0:T(1024)(128)(4,1)} %bitcast.110), calls=%async_computation | async-start | bytes 8388608
  190.9 14.0 %slice-start.2 = ((s8[4718592]{0:T(1024)(128)(4,1)}), s8[4194304]{0:T(1024)(128)(4,1)S(1)}, s32[]{:S(2)}) async-start(s8[4718592]{0:T(1024)(128)(4,1)} %bitcast.116), calls=%async_computation.2 | async-start | bytes 8388608
  192.6 3.7 %collective-permute-start.25 = (f32[8,128]{1,0:T(8,128)S(1)}, f32[8,128]{1,0:T(8,128)S(1)}, u32[]{:S(2)}, u32[]{:S(2)}) collective-permute-start(f32[8,128]{1,0:T(8,128)S(1)} %shard_map.158), channel_id=1, source_target_pairs={{0,4},{4,0},{8,12},{12,8},{16,20},{20,16},{24,28},{28,24},{1,5},{5... | collective-permute-start | bytes 12296 | tf_op jit(solution)/shard_map/ppermute | solution.py:25
  196.3 3.6 %collective-permute-start.26 = (f32[8,128]{1,0:T(8,128)S(1)}, f32[8,128]{1,0:T(8,128)S(1)}, u32[]{:S(2)}, u32[]{:S(2)}) collective-permute-start(f32[8,128]{1,0:T(8,128)S(1)} %add.159), channel_id=1, source_target_pairs={{0,8},{4,12},{8,0},{12,4},{16,24},{20,28},{24,16},{28,20},{1,9},{5... | collective-permute-start | bytes 12296 | tf_op jit(solution)/shard_map/ppermute | solution.py:25
  199.9 4.9 %collective-permute-start.27 = (f32[8,128]{1,0:T(8,128)S(1)}, f32[8,128]{1,0:T(8,128)S(1)}, u32[]{:S(2)}, u32[]{:S(2)}) collective-permute-start(f32[8,128]{1,0:T(8,128)S(1)} %add.160.mine_ref), channel_id=1, source_target_pairs={{0,16},{4,20},{8,24},{12,28},{16,0},{20,4},{24,8},{28,12},{1,17},{... | collective-permute-start | bytes 12296 | tf_op jit(solution)/shard_map/ppermute | solution.py:25
  (13 other events, 64.4 us)

commit v3 on v2

--- a/solution.py
+++ b/solution.py
@@ -189,8 +189,8 @@
     one = pl.Buffered(1)
     whole_spec = pl.BlockSpec((rows, width), whole, pipeline_mode=one)
     in_specs = [
-        whole_spec,
-        whole_spec,
+        pl.BlockSpec(memory_space=pltpu.VMEM),
+        pl.BlockSpec(memory_space=pltpu.VMEM),
         pl.BlockSpec((width, block), column),
         pl.BlockSpec((block, width), row),
     ]

time: 212 us -> 212 us (level)
  no operation moved by 1% of the time
where the time goes in v3:
time: 212 us; the launch traced here: 211 us
  Pallas kernels  73.1 us (34%)
  waiting for transfers between devices  68.8 us (32%)
  starting transfers between devices  35.2 us (17%)
  other arithmetic  20.1 us (9%)
  matrix products  8.51 us (4%)
  local copies, waits for them, and re-layouts  4.32 us (2%)
    ppermute x28, waiting for transfers between devices, swap(): lax.ppermute(x, axis, [(i, i ^ offset) for i in range(lax.axis_size(axis))])  68.8 us
    pallas_call x4, Pallas kernels, expert_call(): pl.pallas_call(functools.partial(expert_kernel, steps=steps, kind=kind),...  62.9 us
    ppermute x28, starting transfers between devices, swap(): lax.ppermute(x, axis, [(i, i ^ offset) for i in range(lax.axis_size(axis))])  35.2 us
    convert_element_type x2, other arithmetic, exchange(): quarter(own, far, other, axis, *pair).astype(f16)  8.32 us
    dot_general x4, matrix products, place_rows(): sent = jnp.dot(table, rows, preferred_element_type=f32).astype(bf16)  6.38 us
    pallas_call x1, Pallas kernels, update_call(): pl.pallas_call(functools.partial(update_kernel, count=count), grid_spec=p...  6.09 us
    another operation x4, other arithmetic  5.09 us
  transfers between devices with their start and end apart: 28, of which 12 were waited for; matrix products, arithmetic and copies ran while one was open for 13% of the time, Pallas kernels for 31%

profile of v3, /device:TPU:0, one launch (start us, length us, event | category | flops | bytes accessed | tf_op | source)
XLA Modules:
  0.0 211.3 jit_solution(13596774176772140527)
XLA Ops:
  0.6 4.1 %collective-permute-start.6 = (s32[4,128]{1,0:T(4,128)}, s32[4,128]{1,0:T(4,128)S(1)}, u32[]{:S(2)}, u32[]{:S(2)}) collective-permute-start(s32[4,128]{1,0:T(4,128)} %bitcast.118), channel_id=1, source_target_pairs={{0,16},{4,20},{8,24},{12,28},{16,0},{20,4},{24,8},{28,12},{1,17},{... | collective-permute-start | bytes 6152 | tf_op jit(solution)/shard_map/ppermute | solution.py:25
  11.8 2.2 %fusion.6 = bf16[1024,768]{1,0:T(8,128)(2,1)S(1)} fusion(bf16[512,768]{1,0:T(8,128)(2,1)} %param.10, s32[512]{0:T(512)S(1)} %multiply_add_fusion.3), kind=kOutput, calls=%fused_computation.8 | convolution fusion | flops 806617088 | bytes 2361344 | tf_op jit(solution)/shard_map/dot_general | solution.py:69
  15.9 2.3 %reduce-window.16 = s32[4,4,128]{2,1,0:T(4,128)S(1)} reduce-window(s32[4,4,128]{2,1,0:T(4,128)} %fusion.30, s32[]{:T(128)} %constant.48.clone.1), window={size=1x1x128 pad=0_0x0_0x127_0}, to_apply=%region_3.4 | reduce-window | flops 260096 | bytes 16388 | tf_op jit(solution)/shard_map/reduce-window.2
  22.9 6.5 %collective-permute-done.5 = bf16[256,768]{1,0:T(8,128)(2,1)S(1)} collective-permute-done((bf16[256,768]{1,0:T(8,128)(2,1)S(1)}, bf16[256,768]{1,0:T(8,128)(2,1)S(1)}, u32[]{:S(2)}, u32[]{:S(2)}) %collective-permute-start.5) | collective-permute-done | bytes 393248 | tf_op jit(solution)/shard_map/ppermute | solution.py:25
  29.6 2.9 %collective-permute-start.8 = (bf16[512,768]{1,0:T(8,128)(2,1)S(1)}, bf16[512,768]{1,0:T(8,128)(2,1)S(1)}, u32[]{:S(2)}, u32[]{:S(2)}) collective-permute-start(bf16[512,768]{1,0:T(8,128)(2,1)S(1)} %copy-done.8), channel_id=1, source_target_pairs={{0,16},{4,20},{8,24},{12,28},{16,0},{20,4},{24,8},{28,12},{1,17},{... | collective-permute-start | bytes 2359304 | tf_op jit(solution)/shard_map/ppermute | solution.py:25
  32.5 6.1 %collective-permute-done.1 = bf16[256,768]{1,0:T(8,128)(2,1)S(1)} collective-permute-done((bf16[256,768]{1,0:T(8,128)(2,1)}, bf16[256,768]{1,0:T(8,128)(2,1)S(1)}, u32[]{:S(2)}, u32[]{:S(2)}) %collective-permute-start.1) | collective-permute-done | bytes 393248 | tf_op jit(solution)/shard_map/ppermute | solution.py:25
  38.6 7.7 %collective-permute-done.2 = bf16[256,768]{1,0:T(8,128)(2,1)S(1)} collective-permute-done((bf16[256,768]{1,0:T(8,128)(2,1)}, bf16[256,768]{1,0:T(8,128)(2,1)S(1)}, u32[]{:S(2)}, u32[]{:S(2)}) %collective-permute-start.2) | collective-permute-done | bytes 393248 | tf_op jit(solution)/shard_map/ppermute | solution.py:25
  47.4 13.6 %shard_map.153 = (f32[384,3072]{1,0:T(8,128)}, f32[768,1536]{1,0:T(8,128)}, f32[1024,768]{1,0:T(8,128)}) custom-call(s32[3]{0:T(128)S(1)} %pad_add_fusion.info_ref, bf16[1024,768]{1,0:T(8,128)(2,1)S(1)} %pad_maximum_fusion.x_ref, bf16[1024,768]{1,0:T(8,128)(2,1)S(1)} %pad_maximum_fusion.1.u_ref, bf16[768,3072]{1,0:T(8,128)(2,1)} %bitcast.106, ...), custom_call_target="tpu_custom_call" | custom-call | flops 1024 | bytes 1024 | tf_op jit(solution)/shard_map/pallas_call | solution.py:226
  61.1 2.2 %fusion.7 = bf16[1024,768]{1,0:T(8,128)(2,1)S(1)} fusion(bf16[512,768]{1,0:T(8,128)(2,1)} %collective-permute-done.7, s32[512]{0:T(512)S(1)} %multiply_add_fusion.2), kind=kOutput, calls=%fused_computation.9 | convolution fusion | flops 806617088 | bytes 2361344 | tf_op jit(solution)/shard_map/dot_general | solution.py:69
  65.6 9.0 %shard_map.154 = (f32[384,3072]{1,0:T(8,128)}, f32[768,1536]{1,0:T(8,128)}, f32[1024,768]{1,0:T(8,128)}) custom-call(s32[3]{0:T(128)S(1)} %pad_add_fusion.info_ref, bf16[1024,768]{1,0:T(8,128)(2,1)S(1)} %pad_maximum_fusion.x_ref, bf16[1024,768]{1,0:T(8,128)(2,1)S(1)} %pad_maximum_fusion.1.u_ref, ...), custom_call_target="tpu_custom_call", output_to_operand_aliasing={{0}: (6, {}), {1}: (7, {})} | custom-call | flops 1024 | bytes 1024 | tf_op jit(solution)/shard_map/pallas_call | solution.py:226
  74.6 2.1 collective-permute-done.8
  79.7 14.9 %shard_map.155 = (f32[384,3072]{1,0:T(8,128)}, bf16[1024,768]{1,0:T(8,128)(2,1)S(1)}) custom-call(s32[3]{0:T(128)S(1)} %pad_add_fusion.info_ref, bf16[1024,768]{1,0:T(8,128)(2,1)S(1)} %pad_maximum_fusion.x_ref, bf16[1024,768]{1,0:T(8,128)(2,1)S(1)} %pad_maximum_fusion.1.u_ref, bf16[768,3072]{1,0:T(8,128)(2,1)} %bitcast.108, ...), custom_call_target="tpu_custom_call", output_to_operand_aliasing={{0}: (6, {})} | custom-call | flops 1024 | bytes 1024 | tf_op jit(solution)/shard_map/pallas_call | solution.py:226
  94.7 5.2 %collective-permute-done.14 = bf16[256,768]{1,0:T(8,128)(2,1)S(1)} collective-permute-done((bf16[256,768]{1,0:T(8,128)(2,1)S(1)}, bf16[256,768]{1,0:T(8,128)(2,1)S(1)}, u32[]{:S(2)}, u32[]{:S(2)}) %collective-permute-start.14) | collective-permute-done | bytes 393248 | tf_op jit(solution)/shard_map/ppermute | solution.py:25
  102.2 25.4 %shard_map.156 = (f32[384,3072]{1,0:T(8,128)}, f32[768,1536]{1,0:T(8,128)}, f32[8,128]{1,0:T(8,128)S(1)}) custom-call(s32[3]{0:T(128)S(1)} %pad_add_fusion.info_ref, bf16[1024,768]{1,0:T(8,128)(2,1)S(1)} %pad_maximum_fusion.3.x_ref, bf16[1024,768]{1,0:T(8,128)(2,1)S(1)} %pad_maximum_fusion.2.u_ref, bf16[768,3072]{1,0:T(8,128)(2,1)} %bitcast.109, ...), custom_call_target="tpu_custom_call" | custom-call | flops 1024 | bytes 1024 | tf_op jit(solution)/shard_map/pallas_call | solution.py:226
  128.5 2.7 %collective-permute-start.18 = (f32[8,128]{1,0:T(8,128)S(1)}, f32[8,128]{1,0:T(8,128)S(1)}, u32[]{:S(2)}, u32[]{:S(2)}) collective-permute-start(f32[8,128]{1,0:T(8,128)S(1)} %get-tuple-element.54), channel_id=1, source_target_pairs={{0,16},{4,20},{8,24},{12,28},{16,0},{20,4},{24,8},{28,12},{1,17},{... | collective-permute-start | bytes 12296 | tf_op jit(solution)/shard_map/ppermute | solution.py:25
  131.2 1.8 collective-permute-done.18
  133.0 3.9 %add_convert_fusion.3 = (f16[96,3072]{1,0:T(8,128)(2,1)S(1)}, f16[96,3072]{1,0:T(8,128)(2,1)S(1)}, f16[96,3072]{1,0:T(8,128)(2,1)S(1)}) fusion(f32[384,3072]{1,0:T(8,128)} %get-tuple-element.55, s32[]{:T(128)S(6)} %select_n.47, f32[384,3072]{1,0:T(8,128)} %get-tuple-element.51.rest_0_, f32[]{:T(128)S(1)} %bitcast.128, f32[]{:T(128)S(1)} %bitcast.123, ...), kind=kLoop, calls=%fused_computation.29 | loop fusion | flops 3538944 | bytes 8847380 | tf_op jit(solution)/shard_map/convert_element_type | solution.py:493
  136.9 1.8 collective-permute-start.19
  140.4 4.5 %add_convert_fusion = (f16[768,384]{1,0:T(8,128)(2,1)S(1)}, f16[768,384]{1,0:T(8,128)(2,1)S(1)}, f16[768,384]{1,0:T(8,128)(2,1)S(1)}, f32[768,384]{1,0:T(8,128)S(1)}) fusion(f32[768,1536]{1,0:T(8,128)} %get-tuple-element.58, s32[]{:T(128)S(6)} %select_n.52, f32[768,1536]{1,0:T(8,128)} %get-tuple-element.52.rest_1_, f32[]{:T(128)S(1)} %bitcast.129, ...), kind=kLoop, calls=%fused_computation.24 | loop fusion | flops 4423680 | bytes 12386328 | tf_op jit(solution)/shard_map/convert_element_type | solution.py:493
  144.9 1.8 collective-permute-start.22
  148.1 16.3 %collective-permute-done.19 = f16[96,3072]{1,0:T(8,128)(2,1)S(1)} collective-permute-done((f16[96,3072]{1,0:T(8,128)(2,1)S(1)}, f16[96,3072]{1,0:T(8,128)(2,1)S(1)}, u32[]{:S(2)}, u32[]{:S(2)}) %collective-permute-start.19) | collective-permute-done | bytes 589856 | tf_op jit(solution)/shard_map/ppermute | solution.py:25
  164.3 2.5 %collective-permute-start.24 = (f16[768,384]{1,0:T(8,128)(2,1)S(1)}, f16[768,384]{1,0:T(8,128)(2,1)S(1)}, u32[]{:S(2)}, u32[]{:S(2)}) collective-permute-start(f16[768,384]{1,0:T(8,128)(2,1)S(1)} %get-tuple-element.70), channel_id=1, source_target_pairs={{0,12},{4,8},{8,4},{12,0},{16,28},{20,24},{24,20},{28,16},{1,13},{... | collective-permute-start | bytes 1769480 | tf_op jit(solution)/shard_map/ppermute | solution.py:25
  166.9 1.8 multiply_add_fusion.1.refs_0_
  169.0 2.4 %shard_map.157.before_ref = f32[8,128]{1,0:T(8,128)S(1)} custom-call(s32[3]{0:T(128)S(1)} %pad_add_fusion.info_ref, f32[1,128]{1,0:T(1,128)S(1)} %rsqrt_multiply_fusion.1.before_ref, f32[96,3072]{1,0:T(8,128)S(1)} %multiply_add_fusion.1.refs_0_, f32[96,3072]{1,0:T(8,128)S(1)} %convert_element_type.87.refs_1_, f32[96,3072]{1,0:T(8,128)S(1)} %convert_element_type.88.refs_2_, ...), custom_call_target="tpu_custom_call" | custom-call | tf_op jit(solution)/shard_map/pallas_call | solution.py:282
  171.4 6.1 %collective-permute-done.22 = f16[768,384]{1,0:T(8,128)(2,1)S(1)} collective-permute-done((f16[768,384]{1,0:T(8,128)(2,1)S(1)}, f16[768,384]{1,0:T(8,128)(2,1)S(1)}, u32[]{:S(2)}, u32[]{:S(2)}) %collective-permute-start.22) | collective-permute-done | bytes 589856 | tf_op jit(solution)/shard_map/ppermute | solution.py:25
  177.6 2.7 %collective-permute-done.23 = f16[768,384]{1,0:T(8,128)(2,1)S(1)} collective-permute-done((f16[768,384]{1,0:T(8,128)(2,1)S(1)}, f16[768,384]{1,0:T(8,128)(2,1)S(1)}, u32[]{:S(2)}, u32[]{:S(2)}) %collective-permute-start.23) | collective-permute-done | bytes 589856 | tf_op jit(solution)/shard_map/ppermute | solution.py:25
  180.3 10.4 %collective-permute-done.24 = f16[768,384]{1,0:T(8,128)(2,1)S(1)} collective-permute-done((f16[768,384]{1,0:T(8,128)(2,1)S(1)}, f16[768,384]{1,0:T(8,128)(2,1)S(1)}, u32[]{:S(2)}, u32[]{:S(2)}) %collective-permute-start.24) | collective-permute-done | bytes 589856 | tf_op jit(solution)/shard_map/ppermute | solution.py:25
  194.3 2.0 collective-permute-done.25
  198.1 1.9 collective-permute-done.26
  199.9 2.7 %collective-permute-start.27 = (f32[8,128]{1,0:T(8,128)S(1)}, f32[8,128]{1,0:T(8,128)S(1)}, u32[]{:S(2)}, u32[]{:S(2)}) collective-permute-start(f32[8,128]{1,0:T(8,128)S(1)} %add.160.mine_ref), channel_id=1, source_target_pairs={{0,16},{4,20},{8,24},{12,28},{16,0},{20,4},{24,8},{28,12},{1,17},{... | collective-permute-start | bytes 12296 | tf_op jit(solution)/shard_map/ppermute | solution.py:25
  202.7 2.1 %multiply_convert_fusion = bf16[512,768]{1,0:T(8,128)(2,1)} fusion(bf16[256,768]{1,0:T(8,128)(2,1)S(1)} %copy-done.12, bf16[256,768]{1,0:T(8,128)(2,1)S(1)} %copy-done.10, bf16[256,768]{1,0:T(8,128)(2,1)S(1)} %collective-permute-done.15, bf16[256,768]{1,0:T(8,128)(2,1)S(1)} %get-tuple-element.77, s32[512]{0:T(512)S(1)} %copy-done.7, f32[512]{0:T(512)S(1)} %bitcast.132), kind=kOutput, calls=%fused_computation.22 | convolution fusion | flops 812908544 | bytes 2363392 | tf_op jit(solution)/shard_map/dot_general | solution.py:47
  205.0 6.1 %shard_map.159 = (f32[1,96,3072]{2,1,0:T(8,128)}, f32[1,384,768]{2,1,0:T(8,128)}, f32[1,96,3072]{2,1,0:T(8,128)}, f32[1,384,768]{2,1,0:T(8,128)}, f32[1,96,3072]{2,1,0:T(8,128)}, /*index=5*/f32[1,384,768]{2,1,0:T(8,128)}) custom-call(s32[3]{0:T(128)S(1)} %pad_add_fusion.info_ref, f32[8,128]{1,0:T(8,128)S(1)} %add.160.mine_ref, ...), custom_call_target="tpu_custom_call" | custom-call | tf_op jit(solution)/shard_map/pallas_call | solution.py:367
  (112 shorter events, 32.6 us)
Async XLA Ops:
  0.6 14.4 %collective-permute-start.6 = (s32[4,128]{1,0:T(4,128)}, s32[4,128]{1,0:T(4,128)S(1)}, u32[]{:S(2)}, u32[]{:S(2)}) collective-permute-start(s32[4,128]{1,0:T(4,128)} %bitcast.118), channel_id=1, source_target_pairs={{0,16},{4,20},{8,24},{12,28},{16,0},{20,4},{24,8},{28,12},{1,17},{... | collective-permute-start | bytes 6152 | tf_op jit(solution)/shard_map/ppermute | solution.py:25
  6.1 55.0 %collective-permute-start.7 = (bf16[512,768]{1,0:T(8,128)(2,1)S(1)}, bf16[512,768]{1,0:T(8,128)(2,1)}, u32[]{:S(2)}, u32[]{:S(2)}) collective-permute-start(bf16[512,768]{1,0:T(8,128)(2,1)S(1)} %multiply_convert_fusion.1), channel_id=1, source_target_pairs={{0,16},{4,20},{8,24},{12,28},{16,0},{20,4},{24,8},{28,12},{1,17},{... | collective-permute-start | bytes 2359304 | tf_op jit(solution)/shard_map/ppermute | solution.py:25
  9.8 11.3 %collective-permute-start.3 = (bf16[256,768]{1,0:T(8,128)(2,1)}, bf16[256,768]{1,0:T(8,128)(2,1)S(1)}, u32[]{:S(2)}, u32[]{:S(2)}) collective-permute-start(bf16[256,768]{1,0:T(8,128)(2,1)} %get-tuple-element.95), channel_id=1, source_target_pairs={{0,1},{1,0},{2,3},{3,2},{4,5},{5,4},{6,7},{7,6},{8,9},{9,8},{10,11... | collective-permute-start | bytes 1179656 | tf_op jit(solution)/shard_map/ppermute | solution.py:25
  9.8 13.1 %collective-permute-start.4 = (bf16[256,768]{1,0:T(8,128)(2,1)S(1)}, bf16[256,768]{1,0:T(8,128)(2,1)S(1)}, u32[]{:S(2)}, u32[]{:S(2)}) collective-permute-start(bf16[256,768]{1,0:T(8,128)(2,1)S(1)} %get-tuple-element.94), channel_id=1, source_target_pairs={{0,2},{1,3},{2,0},{3,1},{4,6},{5,7},{6,4},{7,5},{8,10},{9,11},{10,... | collective-permute-start | bytes 1179656 | tf_op jit(solution)/shard_map/ppermute | solution.py:25
  11.6 17.9 %collective-permute-start.5 = (bf16[256,768]{1,0:T(8,128)(2,1)S(1)}, bf16[256,768]{1,0:T(8,128)(2,1)S(1)}, u32[]{:S(2)}, u32[]{:S(2)}) collective-permute-start(bf16[256,768]{1,0:T(8,128)(2,1)S(1)} %get-tuple-element.93), channel_id=1, source_target_pairs={{0,3},{1,2},{2,1},{3,0},{4,7},{5,6},{6,5},{7,4},{8,11},{9,10},{10,... | collective-permute-start | bytes 1179656 | tf_op jit(solution)/shard_map/ppermute | solution.py:25
  15.0 17.4 %collective-permute-start = (bf16[256,768]{1,0:T(8,128)(2,1)}, bf16[256,768]{1,0:T(8,128)(2,1)}, u32[]{:S(2)}, u32[]{:S(2)}) collective-permute-start(bf16[256,768]{1,0:T(8,128)(2,1)} %get-tuple-element.92), channel_id=1, source_target_pairs={{0,1},{1,0},{2,3},{3,2},{4,5},{5,4},{6,7},{7,6},{8,9},{9,8},{10,11... | collective-permute-start | bytes 1179656 | tf_op jit(solution)/shard_map/ppermute | solution.py:25
  21.1 17.5 %collective-permute-start.1 = (bf16[256,768]{1,0:T(8,128)(2,1)}, bf16[256,768]{1,0:T(8,128)(2,1)S(1)}, u32[]{:S(2)}, u32[]{:S(2)}) collective-permute-start(bf16[256,768]{1,0:T(8,128)(2,1)} %get-tuple-element.91), channel_id=1, source_target_pairs={{0,2},{1,3},{2,0},{3,1},{4,6},{5,7},{6,4},{7,5},{8,10},{9,11},{10,... | collective-permute-start | bytes 1179656 | tf_op jit(solution)/shard_map/ppermute | solution.py:25
  22.9 23.4 %collective-permute-start.2 = (bf16[256,768]{1,0:T(8,128)(2,1)}, bf16[256,768]{1,0:T(8,128)(2,1)S(1)}, u32[]{:S(2)}, u32[]{:S(2)}) collective-permute-start(bf16[256,768]{1,0:T(8,128)(2,1)} %get-tuple-element.90), channel_id=1, source_target_pairs={{0,3},{1,2},{2,1},{3,0},{4,7},{5,6},{6,5},{7,4},{8,11},{9,10},{10,... | collective-permute-start | bytes 1179656 | tf_op jit(solution)/shard_map/ppermute | solution.py:25
  29.6 47.0 %collective-permute-start.8 = (bf16[512,768]{1,0:T(8,128)(2,1)S(1)}, bf16[512,768]{1,0:T(8,128)(2,1)S(1)}, u32[]{:S(2)}, u32[]{:S(2)}) collective-permute-start(bf16[512,768]{1,0:T(8,128)(2,1)S(1)} %copy-done.8), channel_id=1, source_target_pairs={{0,16},{4,20},{8,24},{12,28},{16,0},{20,4},{24,8},{28,12},{1,17},{... | collective-permute-start | bytes 2359304 | tf_op jit(solution)/shard_map/ppermute | solution.py:25
  63.3 16.0 %collective-permute-start.10 = (bf16[256,768]{1,0:T(8,128)(2,1)S(1)}, bf16[256,768]{1,0:T(8,128)(2,1)S(1)}, u32[]{:S(2)}, u32[]{:S(2)}) collective-permute-start(bf16[256,768]{1,0:T(8,128)(2,1)S(1)} %get-tuple-element.86), channel_id=1, source_target_pairs={{0,2},{1,3},{2,0},{3,1},{4,6},{5,7},{6,4},{7,5},{8,10},{9,11},{10,... | collective-permute-start | bytes 1179656 | tf_op jit(solution)/shard_map/ppermute | solution.py:25
  65.1 29.5 %collective-permute-start.11 = (bf16[256,768]{1,0:T(8,128)(2,1)S(1)}, bf16[256,768]{1,0:T(8,128)(2,1)S(1)}, u32[]{:S(2)}, u32[]{:S(2)}) collective-permute-start(bf16[256,768]{1,0:T(8,128)(2,1)S(1)} %get-tuple-element.85), channel_id=1, source_target_pairs={{0,3},{1,2},{2,1},{3,0},{4,7},{5,6},{6,5},{7,4},{8,11},{9,10},{10,... | collective-permute-start | bytes 1179656 | tf_op jit(solution)/shard_map/ppermute | solution.py:25
  65.4 29.2 %collective-permute-start.9 = (bf16[256,768]{1,0:T(8,128)(2,1)S(1)}, bf16[256,768]{1,0:T(8,128)(2,1)S(1)}, u32[]{:S(2)}, u32[]{:S(2)}) collective-permute-start(bf16[256,768]{1,0:T(8,128)(2,1)S(1)} %get-tuple-element.87), channel_id=1, source_target_pairs={{0,1},{1,0},{2,3},{3,2},{4,5},{5,4},{6,7},{7,6},{8,9},{9,8},{10,11... | collective-permute-start | bytes 1179656 | tf_op jit(solution)/shard_map/ppermute | solution.py:25
  77.8 17.0 %collective-permute-start.12 = (bf16[256,768]{1,0:T(8,128)(2,1)S(1)}, bf16[256,768]{1,0:T(8,128)(2,1)S(1)}, u32[]{:S(2)}, u32[]{:S(2)}) collective-permute-start(bf16[256,768]{1,0:T(8,128)(2,1)S(1)} %get-tuple-element.83), channel_id=1, source_target_pairs={{0,1},{1,0},{2,3},{3,2},{4,5},{5,4},{6,7},{7,6},{8,9},{9,8},{10,11... | collective-permute-start | bytes 1179656 | tf_op jit(solution)/shard_map/ppermute | solution.py:25
  77.8 16.9 %collective-permute-start.13 = (bf16[256,768]{1,0:T(8,128)(2,1)S(1)}, bf16[256,768]{1,0:T(8,128)(2,1)S(1)}, u32[]{:S(2)}, u32[]{:S(2)}) collective-permute-start(bf16[256,768]{1,0:T(8,128)(2,1)S(1)} %get-tuple-element.82), channel_id=1, source_target_pairs={{0,2},{1,3},{2,0},{3,1},{4,6},{5,7},{6,4},{7,5},{8,10},{9,11},{10,... | collective-permute-start | bytes 1179656 | tf_op jit(solution)/shard_map/ppermute | solution.py:25
  79.4 20.6 %collective-permute-start.14 = (bf16[256,768]{1,0:T(8,128)(2,1)S(1)}, bf16[256,768]{1,0:T(8,128)(2,1)S(1)}, u32[]{:S(2)}, u32[]{:S(2)}) collective-permute-start(bf16[256,768]{1,0:T(8,128)(2,1)S(1)} %get-tuple-element.81), channel_id=1, source_target_pairs={{0,3},{1,2},{2,1},{3,0},{4,7},{5,6},{6,5},{7,4},{8,11},{9,10},{10,... | collective-permute-start | bytes 1179656 | tf_op jit(solution)/shard_map/ppermute | solution.py:25
  100.2 27.4 %collective-permute-start.15 = (bf16[256,768]{1,0:T(8,128)(2,1)S(1)}, bf16[256,768]{1,0:T(8,128)(2,1)S(1)}, u32[]{:S(2)}, u32[]{:S(2)}) collective-permute-start(bf16[256,768]{1,0:T(8,128)(2,1)S(1)} %get-tuple-element.80), channel_id=1, source_target_pairs={{0,1},{1,0},{2,3},{3,2},{4,5},{5,4},{6,7},{7,6},{8,9},{9,8},{10,11... | collective-permute-start | bytes 1179656 | tf_op jit(solution)/shard_map/ppermute | solution.py:25
  100.4 27.2 %collective-permute-start.16 = (bf16[256,768]{1,0:T(8,128)(2,1)S(1)}, bf16[256,768]{1,0:T(8,128)(2,1)S(1)}, u32[]{:S(2)}, u32[]{:S(2)}) collective-permute-start(bf16[256,768]{1,0:T(8,128)(2,1)S(1)} %get-tuple-element.79), channel_id=1, source_target_pairs={{0,2},{1,3},{2,0},{3,1},{4,6},{5,7},{6,4},{7,5},{8,10},{9,11},{10,... | collective-permute-start | bytes 1179656 | tf_op jit(solution)/shard_map/ppermute | solution.py:25
  102.2 25.4 %collective-permute-start.17 = (bf16[256,768]{1,0:T(8,128)(2,1)S(1)}, bf16[256,768]{1,0:T(8,128)(2,1)S(1)}, u32[]{:S(2)}, u32[]{:S(2)}) collective-permute-start(bf16[256,768]{1,0:T(8,128)(2,1)S(1)} %get-tuple-element.78), channel_id=1, source_target_pairs={{0,3},{1,2},{2,1},{3,0},{4,7},{5,6},{6,5},{7,4},{8,11},{9,10},{10,... | collective-permute-start | bytes 1179656 | tf_op jit(solution)/shard_map/ppermute | solution.py:25
  128.5 4.5 %collective-permute-start.18 = (f32[8,128]{1,0:T(8,128)S(1)}, f32[8,128]{1,0:T(8,128)S(1)}, u32[]{:S(2)}, u32[]{:S(2)}) collective-permute-start(f32[8,128]{1,0:T(8,128)S(1)} %get-tuple-element.54), channel_id=1, source_target_pairs={{0,16},{4,20},{8,24},{12,28},{16,0},{20,4},{24,8},{28,12},{1,17},{... | collective-permute-start | bytes 12296 | tf_op jit(solution)/shard_map/ppermute | solution.py:25
  136.9 27.5 %collective-permute-start.19 = (f16[96,3072]{1,0:T(8,128)(2,1)S(1)}, f16[96,3072]{1,0:T(8,128)(2,1)S(1)}, u32[]{:S(2)}, u32[]{:S(2)}) collective-permute-start(f16[96,3072]{1,0:T(8,128)(2,1)S(1)} %get-tuple-element.76), channel_id=1, source_target_pairs={{0,4},{4,0},{8,12},{12,8},{16,20},{20,16},{24,28},{28,24},{1,5},{5... | collective-permute-start | bytes 1769480 | tf_op jit(solution)/shard_map/ppermute | solution.py:25
  138.7 30.1 %collective-permute-start.20 = (f16[96,3072]{1,0:T(8,128)(2,1)S(1)}, f16[96,3072]{1,0:T(8,128)(2,1)S(1)}, u32[]{:S(2)}, u32[]{:S(2)}) collective-permute-start(f16[96,3072]{1,0:T(8,128)(2,1)S(1)} %get-tuple-element.75), channel_id=1, source_target_pairs={{0,8},{4,12},{8,0},{12,4},{16,24},{20,28},{24,16},{28,20},{1,9},{5... | collective-permute-start | bytes 1769480 | tf_op jit(solution)/shard_map/ppermute | solution.py:25
  140.1 28.8 %collective-permute-start.21 = (f16[96,3072]{1,0:T(8,128)(2,1)S(1)}, f16[96,3072]{1,0:T(8,128)(2,1)S(1)}, u32[]{:S(2)}, u32[]{:S(2)}) collective-permute-start(f16[96,3072]{1,0:T(8,128)(2,1)S(1)} %get-tuple-element.74), channel_id=1, source_target_pairs={{0,12},{4,8},{8,4},{12,0},{16,28},{20,24},{24,20},{28,16},{1,13},{... | collective-permute-start | bytes 1769480 | tf_op jit(solution)/shard_map/ppermute | solution.py:25
  144.9 32.6 %collective-permute-start.22 = (f16[768,384]{1,0:T(8,128)(2,1)S(1)}, f16[768,384]{1,0:T(8,128)(2,1)S(1)}, u32[]{:S(2)}, u32[]{:S(2)}) collective-permute-start(f16[768,384]{1,0:T(8,128)(2,1)S(1)} %get-tuple-element.72), channel_id=1, source_target_pairs={{0,4},{4,0},{8,12},{12,8},{16,20},{20,16},{24,28},{28,24},{1,5},{5... | collective-permute-start | bytes 1769480 | tf_op jit(solution)/shard_map/ppermute | solution.py:25
  146.7 33.6 %collective-permute-start.23 = (f16[768,384]{1,0:T(8,128)(2,1)S(1)}, f16[768,384]{1,0:T(8,128)(2,1)S(1)}, u32[]{:S(2)}, u32[]{:S(2)}) collective-permute-start(f16[768,384]{1,0:T(8,128)(2,1)S(1)} %get-tuple-element.71), channel_id=1, source_target_pairs={{0,8},{4,12},{8,0},{12,4},{16,24},{20,28},{24,16},{28,20},{1,9},{5... | collective-permute-start | bytes 1769480 | tf_op jit(solution)/shard_map/ppermute | solution.py:25
  164.3 26.4 %collective-permute-start.24 = (f16[768,384]{1,0:T(8,128)(2,1)S(1)}, f16[768,384]{1,0:T(8,128)(2,1)S(1)}, u32[]{:S(2)}, u32[]{:S(2)}) collective-permute-start(f16[768,384]{1,0:T(8,128)(2,1)S(1)} %get-tuple-element.70), channel_id=1, source_target_pairs={{0,12},{4,8},{8,4},{12,0},{16,28},{20,24},{24,20},{28,16},{1,13},{... | collective-permute-start | bytes 1769480 | tf_op jit(solution)/shard_map/ppermute | solution.py:25
  180.3 24.5 %copy-start.3 = (f32[1,384,768]{2,1,0:T(8,128)S(1)}, f32[1,384,768]{2,1,0:T(8,128)}, u32[]{:S(2)}) copy-start(f32[1,384,768]{2,1,0:T(8,128)} %refs_13_.1) | copy-start | bytes 3538948
  190.7 11.8 %copy-start.12 = (bf16[256,768]{1,0:T(8,128)(2,1)S(1)}, bf16[256,768]{1,0:T(8,128)(2,1)}, u32[]{:S(2)}) copy-start(bf16[256,768]{1,0:T(8,128)(2,1)} %copy-done.11) | copy-start | bytes 1179652
  190.8 14.0 %slice-start = ((s8[4718592]{0:T(1024)(128)(4,1)}), s8[4194304]{0:T(1024)(128)(4,1)S(1)}, s32[]{:S(2)}) async-start(s8[4718592]{0:T(1024)(128)(4,1)} %bitcast.110), calls=%async_computation | async-start | bytes 8388608
  190.9 14.0 %slice-start.2 = ((s8[4718592]{0:T(1024)(128)(4,1)}), s8[4194304]{0:T(1024)(128)(4,1)S(1)}, s32[]{:S(2)}) async-start(s8[4718592]{0:T(1024)(128)(4,1)} %bitcast.116), calls=%async_computation.2 | async-start | bytes 8388608
  192.6 3.7 %collective-permute-start.25 = (f32[8,128]{1,0:T(8,128)S(1)}, f32[8,128]{1,0:T(8,128)S(1)}, u32[]{:S(2)}, u32[]{:S(2)}) collective-permute-start(f32[8,128]{1,0:T(8,128)S(1)} %shard_map.158), channel_id=1, source_target_pairs={{0,4},{4,0},{8,12},{12,8},{16,20},{20,16},{24,28},{28,24},{1,5},{5... | collective-permute-start | bytes 12296 | tf_op jit(solution)/shard_map/ppermute | solution.py:25
  196.3 3.6 %collective-permute-start.26 = (f32[8,128]{1,0:T(8,128)S(1)}, f32[8,128]{1,0:T(8,128)S(1)}, u32[]{:S(2)}, u32[]{:S(2)}) collective-permute-start(f32[8,128]{1,0:T(8,128)S(1)} %add.159), channel_id=1, source_target_pairs={{0,8},{4,12},{8,0},{12,4},{16,24},{20,28},{24,16},{28,20},{1,9},{5... | collective-permute-start | bytes 12296 | tf_op jit(solution)/shard_map/ppermute | solution.py:25
  199.9 4.9 %collective-permute-start.27 = (f32[8,128]{1,0:T(8,128)S(1)}, f32[8,128]{1,0:T(8,128)S(1)}, u32[]{:S(2)}, u32[]{:S(2)}) collective-permute-start(f32[8,128]{1,0:T(8,128)S(1)} %add.160.mine_ref), channel_id=1, source_target_pairs={{0,16},{4,20},{8,24},{12,28},{16,0},{20,4},{24,8},{28,12},{1,17},{... | collective-permute-start | bytes 12296 | tf_op jit(solution)/shard_map/ppermute | solution.py:25
  (13 other events, 64.4 us)
